TPU v7x, 32 devices: a whole 2x2x4 slice. The times are simulated.
32 devices in a mesh: wide: 8 (over z, core), lev: 4 (over y, x).
Axes of the slice: x: 2, y: 2, z: 4, core: 2. Of those that a mesh axis runs over, the one named last changes fastest.
Arguments:
- zonal_velocity_field: bfloat16 [4, 1280, 2688], P('lev', 'wide'), may hold values from -6 to 6
- meridional_velocity_field: bfloat16 [4, 1280, 2688], P('lev', 'wide'), may hold values from -6 to 6
- thermal_anomaly: bfloat16 [4, 1280, 2688], P('lev', 'wide'), may hold values from -6 to 6
- surface_orography: bfloat16 [1280, 2688], P('wide'), may hold values from -6 to 6
- layer_pressure_depth: float32 [4], replicated, may hold values from 0.2 to 1
- samples_each_circle: int32 [1280], P(('wide', 'lev')), may hold values from 12 to 2576, as said below
- position_zonal_orders: int32 [128], replicated, may hold values from 0 to 127, as said below
- scaled_associated_functions: bfloat16 [64, 640, 256], P(('wide', 'lev')), may hold values from -3 to 3
Outputs:
- spectra: bfloat16 [64, 2, 4, 2, 256], P(('wide', 'lev'))
Inputs may be any that keep to these rules, and one draw needn't show every extreme that they name: `samples_each_circle`: row j has 16 + 4 * (min(j, 1279 - j) + e) points, e one of -1, 0, 1; e = 1 on the two rows next to the equator. `position_zonal_orders`: A permutation of the wavenumbers in which slots 2q and 2q + 1 hold two wavenumbers that add up to 127.
All inputs are finite; a program needn't handle non-finite values.
Results may differ from a plain program's by a relative error of at most 0.0065.
Values may be sent and summed in bfloat16 or wider, within the bound.
A program may use at most 64 MiB of HBM per device.

v0:
```python
import math

import jax
import jax.numpy as jnp
from jax import lax
from jax.sharding import PartitionSpec as P

NF = 2


circle = 2.0 * math.pi


def prefix(part, axis, combine, identity):
    count = lax.axis_size(axis)
    place = lax.axis_index(axis)
    ahead = count - 1 - place
    gathered = lax.all_gather(part, axis)
    state = jnp.zeros_like(part) + jnp.asarray(identity, part.dtype)

    def one(turn, state):
        source = count - 1 - turn
        return combine(state, lax.dynamic_index_in_dim(gathered, source, 0, False))

    return lax.fori_loop(0, ahead, one, state)


def fourier_rows(fields, lengths, waves):
    rows_block = fields.shape[0]
    channels = fields.shape[1]
    sample_tally = fields.shape[2]
    blocks_high = sample_tally // 128
    count = waves.shape[0]
    position = jnp.arange(sample_tally, dtype=jnp.int32)
    masked = jnp.where(
        position[None, None, :] < lengths[:, None, None], fields.astype(jnp.float32), 0.0
    )
    masked = masked.reshape(rows_block, channels, blocks_high, 128)
    lengths_float = lengths.astype(jnp.float32)
    lower_index = jnp.arange(128, dtype=jnp.int32)
    inner_phase = lower_index[None, :, None] * waves[None, None, :] % lengths[:, None, None]
    inner_angle = inner_phase.astype(jnp.float32) * circle / lengths_float[:, None, None]
    inner_table = jnp.concatenate([jnp.cos(inner_angle), jnp.sin(inner_angle)], axis=2)
    partial_sums = jnp.einsum(
        "rcha,ram->rchm", masked, inner_table, precision=lax.Precision.HIGHEST
    )
    part_cos = partial_sums[..., :count]
    part_sin = partial_sums[..., count:]
    upper_index = jnp.arange(blocks_high, dtype=jnp.int32) * 128
    outer_phase = upper_index[None, :, None] * waves[None, None, :] % lengths[:, None, None]
    outer_angle = outer_phase.astype(jnp.float32) * circle / lengths_float[:, None, None]
    outer_cos = jnp.cos(outer_angle)[:, None]
    outer_sin = jnp.sin(outer_angle)[:, None]
    real_part = jnp.sum(part_cos * outer_cos - part_sin * outer_sin, axis=2)
    imag_part = -jnp.sum(part_cos * outer_sin + part_sin * outer_cos, axis=2)
    keep = 2 * waves[None, :] < lengths[:, None]
    factor = jnp.where(keep, 1.0 / lengths_float[:, None], 0.0)[:, None, :]
    return jnp.stack([real_part * factor, imag_part * factor], axis=1)


def fourier_blocked(fields, lengths, waves):
    total_rows = fields.shape[0]
    shaped = fields.reshape(total_rows, 1, fields.shape[1], fields.shape[2])
    len_shaped = lengths.reshape(total_rows, 1)
    result = lax.map(lambda item: fourier_rows(item[0], item[1], waves), (shaped, len_shaped))
    return result.reshape(total_rows, 2, fields.shape[1], waves.shape[0])


def legendre_pair(data, table, first_wave, waves_total):
    half = table.shape[0]
    width = table.shape[1]
    north_rows = data[:half].astype(jnp.float32)
    south_rows = data[half:][::-1].astype(jnp.float32)
    even_part = (north_rows + south_rows).astype(jnp.bfloat16)
    odd_part = (north_rows - south_rows).astype(jnp.bfloat16)
    stacked = jnp.stack(
        [even_part[..., 0], odd_part[..., 0], even_part[..., 1], odd_part[..., 1]], axis=1
    )
    stacked = stacked.reshape(half, -1)
    product = jnp.dot(stacked.T, table, preferred_element_type=jnp.float32).reshape(4, -1, width)
    column = jnp.arange(width, dtype=jnp.int32)
    split_at = waves_total - first_wave
    in_first = column < split_at
    in_second = jnp.logical_and(column >= split_at, column <= waves_total)
    chosen = jnp.where(in_first, column % 2, 2 + (column - split_at) % 2)
    picked = product[3]
    picked = jnp.where(chosen == 2, product[2], picked)
    picked = jnp.where(chosen == 1, product[1], picked)
    picked = jnp.where(chosen == 0, product[0], picked)
    result = jnp.where(jnp.logical_or(in_first, in_second), picked, 0.0)
    return result.reshape(2, data.shape[2], data.shape[3], width)


def add_terms(earlier, later):
    return earlier + later


def local(
    zonal_velocity_field,
    meridional_velocity_field,
    thermal_anomaly,
    surface_orography,
    layer_pressure_depth,
    samples_each_circle,
    position_zonal_orders,
    scaled_associated_functions,
):
    lev_count = lax.axis_size("lev")
    wide_count = lax.axis_size("wide")
    lev_index = lax.axis_index("lev")
    device_layer_tally = thermal_anomaly.shape[0]
    parallel_strip_circles = thermal_anomaly.shape[1]
    sample_tally = thermal_anomaly.shape[2]
    rows_here = parallel_strip_circles // lev_count
    layer_depth = lax.dynamic_slice_in_dim(
        layer_pressure_depth, lev_index * device_layer_tally, device_layer_tally
    )
    thermal_anomaly_single = thermal_anomaly.astype(jnp.float32)
    quadrature_scaled = thermal_anomaly_single * layer_depth[:, None, None]
    column_part = jnp.sum(quadrature_scaled, axis=0)
    below = prefix(column_part, "lev", add_terms, jnp.zeros_like(column_part))
    local_geo = (
        surface_orography.astype(jnp.float32)[None]
        + jnp.cumsum(quadrature_scaled[::-1], axis=0)[::-1]
    )
    geopotential = local_geo + below[None]
    east = zonal_velocity_field.astype(jnp.float32)
    northern_half = meridional_velocity_field.astype(jnp.float32)
    energy_band = (geopotential + 0.5 * (east * east + northern_half * northern_half)).astype(
        jnp.bfloat16
    )
    transport_product_strip = (northern_half * thermal_anomaly_single).astype(jnp.bfloat16)
    grid_energy, grid_flux = (
        lax.all_to_all(energy_band, "lev", split_axis=1, concat_axis=0, tiled=True),
        lax.all_to_all(transport_product_strip, "lev", split_axis=1, concat_axis=0, tiled=True),
    )
    levels_all = grid_energy.shape[0]
    fields = (
        jnp.stack([grid_energy, grid_flux], axis=1)
        .transpose(2, 0, 1, 3)
        .reshape(rows_here, levels_all * NF, sample_tally)
    )
    coefficients = fourier_blocked(fields, samples_each_circle, position_zonal_orders).reshape(
        rows_here, 2, levels_all, NF, -1
    )
    coefficients = coefficients.astype(jnp.bfloat16)
    sectioned = lax.all_to_all(
        lax.all_to_all(coefficients, "wide", split_axis=4, concat_axis=0, tiled=True),
        "lev",
        split_axis=4,
        concat_axis=0,
        tiled=True,
    )
    slot_count = sectioned.shape[4]
    sectioned = sectioned.reshape(lev_count, wide_count, rows_here, 2, levels_all, NF, slot_count)
    by_pair = sectioned.transpose(1, 0, 2, 3, 4, 5, 6).reshape(
        lev_count * wide_count * rows_here, 2, levels_all, NF, slot_count
    )
    device = lax.axis_index("wide") * lev_count + lev_index
    pairs_here = scaled_associated_functions.shape[0]
    my_slots = lax.dynamic_slice_in_dim(
        position_zonal_orders, device * (2 * pairs_here), 2 * pairs_here
    )
    firsts = my_slots.reshape(pairs_here, 2)[:, 0]
    total_rows = by_pair.shape[0]
    paired = by_pair.reshape(total_rows, 2, levels_all, NF, pairs_here, 2).transpose(
        4, 0, 1, 2, 3, 5
    )
    waves_total = position_zonal_orders.shape[0]
    result = lax.map(
        lambda item: legendre_pair(item[0], item[1], item[2], waves_total),
        (paired, scaled_associated_functions, firsts),
    )
    return result.astype(jnp.bfloat16)


def solution(mesh):
    in_specs = (
        P("lev", "wide", None),
        P("lev", "wide", None),
        P("lev", "wide", None),
        P("wide", None),
        P(),
        P(("wide", "lev")),
        P(),
        P(("wide", "lev"), None, None),
    )
    out_specs = P(("wide", "lev"), None, None, None, None)
    return jax.shard_map(local, mesh=mesh, in_specs=in_specs, out_specs=out_specs, check_vma=False)
```

profile of v0, /device:TPU:0, one launch (start us, length us, event | category | flops | bytes accessed | tf_op | source)
XLA Modules:
  0.0 448.0 jit_solution(1069317923032873038)
XLA Ops:
  7.8 3.2 convert_multiply_fusion.2
  11.1 77.9 %all-gather.2.cloned.1.call-done = f32[4,160,2688]{2,1,0:T(8,128)} async-done(((f32[1,160,2688]{2,1,0:T(8,128)}), f32[4,160,2688]{2,1,0:T(8,128)}) %all-gather.2.cloned.1.call-update) | async-done | bytes 6881296 | tf_op jit(solution)/shard_map/all_gather | solution.py:18
  89.1 5.5 %while.34 = (s32[]{:T(128)}, f32[160,2688]{1,0:T(8,128)S(1)}, s32[]{:T(128)}, f32[4,160,2688]{2,1,0:T(8,128)}, s32[]{:T(128)}, /*index=5*/s32[]{:T(128)}, s32[]{:T(128)}, s32[]{:T(128)}) while((s32[]{:T(128)}, f32[160,2688]{1,0:T(8,128)S(1)}, s32[]{:T(128)}, f32[4,160,2688]{2,1,0:T(8,128)}, s32[]{:T(128)}, /*index=5*/s32[]{:T(128)}, ...), condition=%wide.region_1.2_spmd, body=%wide.region_0.0_spmd.sunk | while | flops 430086 | bytes 5161095 | solution.py:25
  89.1 1.8 bitcast_add_fusion.2
  91.0 1.8 bitcast_add_fusion.2
  92.8 1.8 bitcast_add_fusion.2
  94.6 3.4 fusion.36
  99.8 5.9 %reduce.5 = bf16[160,2688]{1,0:T(8,128)(2,1)S(1)} reduce(bf16[160,1,2688]{2,1,0:T(2,128)(2,1)S(1)} %bitcast.132, bf16[]{:T(256)} %broadcast.510), dimensions={1}, to_apply=%bitcast.91.reduce_sub_computation | reduce | bytes 1720322
  105.7 1.6 reshape.508
  107.3 3.7 all-to-all-start
  112.3 5.9 %reduce.4 = bf16[160,2688]{1,0:T(8,128)(2,1)S(1)} reduce(bf16[160,1,2688]{2,1,0:T(2,128)(2,1)S(1)} %bitcast.133, bf16[]{:T(256)} %broadcast.510), dimensions={1}, to_apply=%bitcast.90.reduce_sub_computation | reduce | bytes 1720322
  118.2 1.6 reshape.506
  119.8 2.9 all-to-all-done
  122.7 3.5 all-to-all-start.1
  127.0 10.3 %all-to-all-done.1 = bf16[4,2,53760]{2,1,0:T(2,128)(2,1)S(1)} async-done(((bf16[4,2,53760]{2,1,0:T(2,128)(2,1)}), bf16[4,2,53760]{2,1,0:T(2,128)(2,1)S(1)}, u32[]{:S(2)}, u32[]{:S(2)}) %all-to-all-start.1) | async-done | bytes 860192 | tf_op jit(solution)/shard_map/all_to_all | solution.py:135
  139.3 269.8 %while.35 = (s32[]{:T(128)}, bf16[40,1,2,8,128]{4,3,2,1,0:T(8,128)(2,1)S(1)}, s32[40,1]{0,1:T(1,128)S(1)}, bf16[40,1,8,2688]{3,2,1,0:T(8,128)(2,1)S(1)}, s32[128...) while((s32[]{:T(128)}, ...), condition=%wide.region_5.6_spmd, body=%wide.region_2.5_spmd.sunk | while | flops 66537624 | bytes 901222 | solution.py:65
  141.2 1.6 fusion.55
  147.9 1.6 fusion.55
  168.2 1.6 fusion.55
  410.4 11.6 %all_to_all.51 = bf16[8,2,5120]{2,1,0:T(2,128)(2,1)S(1)} all-to-all(bf16[8,2,5120]{2,1,0:T(2,128)(2,1)S(1)} %reshape.510), channel_id=1, replica_groups=mesh['wide'=8,'lev'=4] {'wide'}, dimensions={0} | all-to-all | bytes 327680 | tf_op jit(solution)/shard_map/all_to_all | solution.py:148
  423.1 1.6 reshape.504
  424.7 3.5 all-to-all-start.3
  428.5 4.9 %all-to-all-done.3 = bf16[320,2,4,2,16]{0,3,2,1,4:T(2,128)(2,1)S(1)} async-done(((bf16[320,2,4,2,16]{0,3,2,1,4:T(2,128)(2,1)}), bf16[320,2,4,2,16]{0,3,2,1,4:T(2,128)(2,1)S(1)}, u32[]{:S(2)}, u32[]{:S(2)}) %all-to-all-start.3) | async-done | bytes 163872 | tf_op jit(solution)/shard_map/all_to_all | solution.py:147
  435.4 5.1 %while.36 = (s32[]{:T(128)}, bf16[2,2,4,2,256]{4,3,2,1,0:T(2,128)(2,1)S(1)}, s32[2]{0:T(128)S(1)}, bf16[2,1280,2,4,2,2]{1,5,0,4,3,2:T(2,128)(2,1)S(1)}, bf16[2,6...) while((s32[]{:T(128)}, bf16[2,2,4,2,256]{4,3,2,1,0:T(2,128)(2,1)S(1)}, ...), condition=%wide.region_7.8_spmd, body=%wide.region_6.7_spmd.sunk | while | flops 21246212 | bytes 1764505 | solution.py:170
  (511 shorter events, 201.8 us)
Async XLA Ops:
  6.5 82.4 %all-gather.2.cloned.1.call-start = ((), (), s32[]{:S(2)}) async-start(), calls=%async_computation.4 | async-start | bytes 8601600 | tf_op jit(solution)/shard_map/all_gather | solution.py:18
  107.3 15.4 %all-to-all-start = ((bf16[4,2,53760]{2,1,0:T(2,128)(2,1)}), bf16[4,2,53760]{2,1,0:T(2,128)(2,1)S(1)}, u32[]{:S(2)}, u32[]{:S(2)}) async-start(bf16[4,2,53760]{2,1,0:T(2,128)(2,1)} %reshape.508), calls=%async_computation | async-start | bytes 1720320 | tf_op jit(solution)/shard_map/all_to_all | solution.py:134
  122.7 14.6 %all-to-all-start.1 = ((bf16[4,2,53760]{2,1,0:T(2,128)(2,1)}), bf16[4,2,53760]{2,1,0:T(2,128)(2,1)S(1)}, u32[]{:S(2)}, u32[]{:S(2)}) async-start(bf16[4,2,53760]{2,1,0:T(2,128)(2,1)} %reshape.506), calls=%async_computation.1 | async-start | bytes 1720320 | tf_op jit(solution)/shard_map/all_to_all | solution.py:135
  138.4 0.9 copy-start.1
  138.4 0.9 copy-start.2
  138.4 0.9 copy-start.3
  424.7 10.8 %copy-start = (bf16[2,640,256]{2,1,0:T(8,128)(2,1)S(1)}, bf16[2,640,256]{2,1,0:T(8,128)(2,1)}, u32[]{:S(2)}) copy-start(bf16[2,640,256]{2,1,0:T(8,128)(2,1)} %param.21) | copy-start | bytes 1966084
  424.7 8.7 %all-to-all-start.3 = ((bf16[320,2,4,2,16]{0,3,2,1,4:T(2,128)(2,1)}), bf16[320,2,4,2,16]{0,3,2,1,4:T(2,128)(2,1)S(1)}, u32[]{:S(2)}, u32[]{:S(2)}) async-start(bf16[320,2,4,2,16]{0,3,2,1,4:T(2,128)(2,1)} %reshape.504), calls=%async_computation.3 | async-start | bytes 393216 | tf_op jit(solution)/shard_map/all_to_all | solution.py:147
  440.6 0.6 copy-start.4
Sparse Core Ops, SparseCore 0:
  11.2 77.7 all-gather.1
where the time goes:
time: 451 us; the launch traced here: 448 us
  other arithmetic  202 us (45%)
  waiting for transfers between devices  95.9 us (21%)
  loops' own time  81.2 us (18%)
  local copies, waits for them, and re-layouts  20.1 us (4%)
  between operations  13.7 us (3%)
  matrix products  12.8 us (3%)
  blocking collectives  11.6 us (3%)
  starting transfers between devices  10.7 us (2%)
    another operation x1, loops' own time, fourier_blocked(): lax.map(lambda item: fourier_rows(item[0], item[1], waves), (shaped, len_...  79.6 us
    all_gather x1, waiting for transfers between devices, prefix(): gathered = lax.all_gather(part, axis)  77.9 us
    cos x40, other arithmetic, fourier_rows(): jnp.cos(inner_angle)  62 us
    cos x40, other arithmetic, fourier_rows(): outer_cos = jnp.cos(outer_angle)[:, None]  36 us
    convert_element_type x40, other arithmetic, fourier_rows(): lengths_float = lengths.astype(jnp.float32)  25.9 us
    lt x40, other arithmetic, fourier_rows(): position[None, None, :] < lengths[:, None, None]  25.3 us
    select_n x40, other arithmetic, fourier_rows(): factor = jnp.where(keep, 1.0 / lengths_float[:, None], 0.0)[:, None, :]  24.9 us
    dot_general x40, matrix products, fourier_rows(): jnp.einsum('rcha,ram->rchm', masked, inner_table, precision=lax.Precision...  12.4 us
  transfers between devices with their start and end apart: 4, of which 4 were waited for; matrix products, arithmetic and copies ran while one was open for 2% of the time, Pallas kernels for 0%

commit v1 on v0

v1 whole, which is shorter than its diff:
```python
import functools

import jax
import jax.numpy as jnp
from jax import lax
from jax.experimental import pallas as pl
from jax.experimental.pallas import tpu as pltpu
from jax.sharding import PartitionSpec as P

STRIP = 16
LANES = 128
COS = (0.9999992251396179, -19.738981246948242, 64.92865753173828, -85.27162170410156, 58.79049301147461, -21.07110595703125)
SIN = (6.283185005187988, -41.341590881347656, 81.59994506835938, -76.61447143554688, 41.3428840637207, -12.471243858337402)


def horner(coefs, z):
    value = jnp.full_like(z, coefs[-1])
    for c in coefs[-2::-1]:
        value = value * z + c
    return value


def unit(n, length, inverse):
    turns = jnp.round(n * inverse)
    t = (n - turns * length) * inverse
    z = t * t
    return horner(COS, z), t * horner(SIN, z)


def times(a, b):
    return a[0] * b[0] - a[1] * b[1], a[0] * b[1] + a[1] * b[0]


def transform(high, high_pad, lens, scale, waves, lens_col, u, v, temp, oro, out, spread, sums, gathered):
    step = pl.program_id(0)
    steps = pl.num_programs(0)
    rows = steps * STRIP
    south = lax.axis_index("wide") * 2 >= lax.axis_size("wide")
    depth = scale[0]
    ground = scale[1]
    limit = jnp.broadcast_to(lens_col[...], (STRIP, LANES))
    lane = lax.broadcasted_iota(jnp.int32, (STRIP, LANES), 1)
    for h in range(high_pad):
        at = pl.ds(h * STRIP, STRIP)
        if h >= high:
            for c in range(3):
                spread[c, at, :] = jnp.zeros((STRIP, LANES), jnp.float32)
            continue
        cols = pl.ds(h * LANES, LANES)
        east = u[:, cols].astype(jnp.float32)
        north = v[:, cols].astype(jnp.float32)
        heat = temp[:, cols].astype(jnp.float32)
        weighted = heat * depth + oro[:, cols].astype(jnp.float32) * ground
        energy = 0.5 * (east * east + north * north) + weighted
        inside = lane + h * LANES < limit
        spread[0, at, :] = jnp.where(inside, energy, 0.0)
        spread[1, at, :] = jnp.where(inside, weighted, 0.0)
        spread[2, at, :] = jnp.where(inside, north * heat, 0.0)

    sub = lax.broadcasted_iota(jnp.int32, (8, LANES), 0).astype(jnp.float32)
    chunks = waves.shape[1] // LANES
    for chunk in range(chunks):
        m = jnp.broadcast_to(waves[:, chunk * LANES:(chunk + 1) * LANES], (8, LANES))

        def one_row(r, carry):
            length = lens[0, step * STRIP + r]
            inverse = lens[1, step * STRIP + r]
            data = jnp.concatenate(
                [spread[c, pl.ds(r, high_pad, stride=STRIP), :] for c in range(3)], axis=0
            ).astype(jnp.bfloat16)
            tiles = [unit(m * sub, length, inverse)]
            turn = unit(m * 8.0, length, inverse)
            while len(tiles) < LANES // 8:
                tiles = tiles + [times(tile, turn) for tile in tiles]
                turn = times(turn, turn)
            table = jnp.concatenate(
                [
                    jnp.concatenate([tile[0] for tile in tiles], axis=0),
                    jnp.concatenate([tile[1] for tile in tiles], axis=0),
                ],
                axis=1,
            ).astype(jnp.bfloat16)
            part = jnp.dot(data, table, preferred_element_type=jnp.float32)
            outer = [
                unit(m * (sub * float(LANES) + float(8 * LANES * g)), length, inverse)
                for g in range(high_pad // 8)
            ]
            place = jnp.where(south, STRIP - 1 - r, r)
            for c in range(3):
                real = jnp.zeros((8, LANES), jnp.float32)
                imag = jnp.zeros((8, LANES), jnp.float32)
                for g in range(high_pad // 8):
                    base = c * high_pad + g * 8
                    pc = part[base:base + 8, :LANES]
                    ps = part[base:base + 8, LANES:]
                    oc, os = outer[g]
                    real = real + (pc * oc - ps * os)
                    imag = imag - (pc * os + ps * oc)
                at = pl.ds(pl.multiple_of(place * 8, 8), 8)
                sums[2 * c, at, :] = real
                sums[2 * c + 1, at, :] = imag
            return carry

        lax.fori_loop(0, STRIP, one_row, 0, unroll=4)

        block = jnp.where(south, steps - 1 - step, step) * STRIP
        lens_here = jnp.broadcast_to(lens_col[...], (STRIP, LANES)).astype(jnp.float32)
        backward = lax.broadcasted_iota(jnp.int32, (STRIP, LANES), 0)
        m16 = jnp.broadcast_to(waves[:, chunk * LANES:(chunk + 1) * LANES], (STRIP, LANES))
        factor = jnp.zeros((STRIP, LANES), jnp.float32)
        for r in range(STRIP):
            length = lens[0, step * STRIP + r]
            inverse = lens[1, step * STRIP + r]
            place = jnp.where(south, STRIP - 1 - r, r)
            factor = jnp.where(
                backward == place, jnp.where(2.0 * m16 < length, inverse, 0.0), factor
            )
        for k in range(6):
            total = sums[k, pl.ds(0, STRIP, stride=8), :]
            for s in range(1, 8):
                total = total + sums[k, pl.ds(s, STRIP, stride=8), :]
            at = pl.ds(pl.multiple_of(k * rows + block, STRIP), STRIP)
            gathered[chunk, at, :] = total * factor

    @pl.when(step == 0)
    def _():
        tail = gathered.shape[1] - 6 * rows
        if tail:
            for chunk in range(chunks):
                gathered[chunk, 6 * rows:, :] = jnp.zeros((tail, LANES), jnp.float32)

    @pl.when(step == steps - 1)
    def _():
        for chunk in range(chunks):
            for b in range(gathered.shape[1] // LANES):
                out[chunk * LANES:(chunk + 1) * LANES, b * LANES:(b + 1) * LANES] = (
                    gathered[chunk, b * LANES:(b + 1) * LANES, :].T.astype(out.dtype)
                )


def local(u, v, temp, oro, depths, lens, orders, table):
    lev_count = lax.axis_size("lev")
    wide_count = lax.axis_size("wide")
    lev = lax.axis_index("lev")
    wide = lax.axis_index("wide")
    rows = temp.shape[1]
    samples = temp.shape[2]
    waves_total = orders.shape[0]
    high = samples // LANES
    high_pad = -(-high // 8) * 8
    steps = rows // STRIP
    packed = -(-6 * rows // LANES) * LANES
    band = lax.all_gather(lens, "lev", tiled=True)
    band_float = band.astype(jnp.float32)
    scale = jnp.stack(
        [lax.dynamic_index_in_dim(depths, lev, 0, False), (lev == lev_count - 1).astype(jnp.float32)]
    )
    smem = pl.BlockSpec(memory_space=pltpu.SMEM)
    field = pl.BlockSpec((STRIP, samples), lambda i: (i, 0))
    field3 = pl.BlockSpec((None, STRIP, samples), lambda i: (0, i, 0))
    coefs = pl.pallas_call(
        functools.partial(transform, high, high_pad),
        grid=(steps,),
        out_shape=jax.ShapeDtypeStruct((waves_total, packed), jnp.bfloat16),
        in_specs=[
            smem,
            smem,
            pl.BlockSpec((1, waves_total), lambda i: (0, 0)),
            pl.BlockSpec((STRIP, 1), lambda i: (i, 0)),
            field3,
            field3,
            field3,
            field,
        ],
        out_specs=pl.BlockSpec((waves_total, packed), lambda i: (0, 0)),
        scratch_shapes=[
            pltpu.VMEM((3, high_pad * STRIP, LANES), jnp.float32),
            pltpu.VMEM((6, STRIP * 8, LANES), jnp.float32),
            pltpu.VMEM((waves_total // LANES, packed, LANES), jnp.float32),
        ],
        compiler_params=pltpu.CompilerParams(vmem_limit_bytes=40 * 2**20),
    )(
        jnp.stack([band_float, 1.0 / band_float]),
        scale,
        orders.astype(jnp.float32)[None],
        band[:, None],
        u,
        v,
        temp,
        oro,
    )
    devices = lev_count * wide_count
    slots = waves_total // devices
    got = lax.all_to_all(
        coefs.reshape(devices, slots, packed), ("wide", "lev"), split_axis=0, concat_axis=0, tiled=True
    )
    got = got[:, :, :6 * rows].astype(jnp.float32)
    got = got.reshape(wide_count, lev_count, slots, 3, 2, rows)
    under = got[:, :, :, 1]
    below = jnp.cumsum(under[:, ::-1], axis=1)[:, ::-1] - under
    fields = jnp.stack([got[:, :, :, 0] + below, got[:, :, :, 2]], axis=3)
    half = wide_count // 2
    upper = fields[:half]
    lower = fields[half:][::-1]
    both = jnp.stack([upper + lower, upper - lower], axis=0).astype(jnp.bfloat16)
    both = both.transpose(3, 0, 5, 2, 4, 1, 6)
    pairs = slots // 2
    width = table.shape[2]
    both = both.reshape(pairs, -1, half * rows)
    product = jnp.einsum("pkj,pjc->pkc", both, table, preferred_element_type=jnp.float32)
    product = product.reshape(pairs, 4, 2, lev_count, 2, width)
    mine = lax.dynamic_slice_in_dim(orders, (wide * lev_count + lev) * slots, slots)
    first = mine.reshape(pairs, 2)[:, :1]
    column = jnp.arange(width, dtype=jnp.int32)[None]
    split = waves_total - first
    chosen = jnp.where(column < split, column % 2, 2 + (column - split) % 2)
    chosen = jnp.where(column <= waves_total, chosen, 4)[:, None, None, None, :]
    result = jnp.zeros_like(product[:, 0])
    for k in range(4):
        result = jnp.where(chosen == k, product[:, k], result)
    return result.astype(jnp.bfloat16)


def solution(mesh):
    in_specs = (
        P("lev", "wide", None),
        P("lev", "wide", None),
        P("lev", "wide", None),
        P("wide", None),
        P(),
        P(("wide", "lev")),
        P(),
        P(("wide", "lev"), None, None),
    )
    out_specs = P(("wide", "lev"), None, None, None, None)
    return jax.shard_map(local, mesh=mesh, in_specs=in_specs, out_specs=out_specs, check_vma=False)
```

time: 451 us -> 55.9 us (0.12)
  other arithmetic: 202 us -> 4.52 us
  waiting for transfers between devices: 95.9 us -> 10.6 us
  loops' own time: 81.2 us -> 0 us
  Pallas kernels: 0 us -> 13.8 us
  between operations: 13.7 us -> 0.86 us
  matrix products: 12.8 us -> 0.24 us
  local copies, waits for them, and re-layouts: 20.1 us -> 11.8 us
  starting transfers between devices: 10.7 us -> 4.92 us
    cos x80 -> x0, other arithmetic: 98 us -> none  [the longest x40 62 us: fourier_rows(): jnp.cos(inner_angle)]
    another operation x3 -> x0, loops' own time: 81.2 us -> none  [the longest x1 79.6 us: fourier_blocked(): lax.map(lambda item: fourier_rows(item[0], item[1], waves), (shaped, len_...]
    all_gather x1 -> x0, waiting for transfers between devices: 77.9 us -> none  [prefix(): gathered = lax.all_gather(part, axis)]
    convert_element_type x43 -> x2, other arithmetic: 29.3 us -> 0.66 us  [the longest x1 0.65 us: local(): return result.astype(jnp.bfloat16)]
    select_n x80 -> x1, other arithmetic: 25.7 us -> 0.01 us  [local(): chosen = jnp.where(column < split, column % 2, 2 + (column - split) % 2)]
    lt x40 -> x0, other arithmetic: 25.3 us -> none  [fourier_rows(): position[None, None, :] < lengths[:, None, None]]
    pallas_call x0 -> x1, Pallas kernels: none -> 13.8 us  [local(): pl.pallas_call(functools.partial(transform, high, high_pad), grid=(steps,...]
    dot_general x42 -> x1, matrix products: 12.8 us -> 0.24 us  [local(): jnp.einsum('pkj,pjc->pkc', both, table, preferred_element_type=jnp.float32)]
  transfers between devices with their start and end apart: 4 -> 1, of which waited for: 4 -> 1; matrix products, arithmetic and copies ran while one was open for 2% -> 1% of each run, Pallas kernels for 0% -> 0%
where the time goes in v1:
time: 55.9 us; the launch traced here: 55.5 us
  Pallas kernels  13.8 us (25%)
  local copies, waits for them, and re-layouts  11.8 us (21%)
  waiting for transfers between devices  10.6 us (19%)
  blocking collectives  8.82 us (16%)
  starting transfers between devices  4.92 us (9%)
  other arithmetic  4.52 us (8%)
  between operations  0.86 us (2%)
    pallas_call x1, Pallas kernels, local(): pl.pallas_call(functools.partial(transform, high, high_pad), grid=(steps,...  13.8 us
    all_to_all x1, waiting for transfers between devices, local(): lax.all_to_all(coefs.reshape(devices, slots, packed), ('wide', 'lev'), sp...  10.6 us
    unnamed x1, blocking collectives  8.82 us
    unnamed x23, local copies, waits for them, and re-layouts  8.27 us
    all_to_all x1, starting transfers between devices, local(): lax.all_to_all(coefs.reshape(devices, slots, packed), ('wide', 'lev'), sp...  4.92 us
    another operation x1, other arithmetic, local(): below = jnp.cumsum(under[:, ::-1], axis=1)[:, ::-1] - under  2.27 us
  transfers between devices with their start and end apart: 1, of which 1 were waited for; matrix products, arithmetic and copies ran while one was open for 1% of the time, Pallas kernels for 0%

profile of v1, /device:TPU:0, one launch (start us, length us, event | category | flops | bytes accessed | tf_op | source)
XLA Modules:
  0.0 55.5 jit_solution(2506631990299246563)
XLA Ops:
  0.0 0.7 %copy-done.8 = u32[32]{0:T(128)S(1)} copy-done((u32[32]{0:T(128)S(1)}, u32[32]{0:T(128)}, u32[]{:S(2)}) %copy-start.8) | copy-done | bytes 152
  0.7 0.6 %dynamic-slice = u32[1]{0:T(128)} dynamic-slice(u32[32]{0:T(128)S(1)} %copy-done.8, u32[]{:T(128)S(6)} %add.71), dynamic_slice_sizes={1} | dynamic-slice | bytes 12
  2.0 0.6 %copy-done.5 = s32[40]{0:T(128)S(1)} copy-done((s32[40]{0:T(128)S(1)}, s32[40]{0:T(128)}, u32[]{:S(2)}) %copy-start.5) | copy-done | bytes 184
  2.8 8.8 %all-reduce = s32[160]{0:T(256)S(1)} all-reduce(s32[160]{0:T(256)S(1)} %dynamic-update-slice), channel_id=1, replica_groups=mesh['wide'=8,'lev'=4] {'lev'}, use_global_device_ids=true, to_apply=%add | all-reduce | flops 160 | bytes 1280
  11.8 0.5 copy-done.7
  12.3 0.7 %copy-done.6 = f32[4]{0:T(128)S(1)} copy-done((f32[4]{0:T(128)S(1)}, f32[4]{0:T(128)}, u32[]{:S(2)}) %copy-start.6) | copy-done | bytes 40
  13.0 0.6 %dynamic_slice.8 = f32[1]{0:T(128)} dynamic-slice(f32[4]{0:T(128)S(1)} %copy-done.6, s32[]{:T(128)S(6)} %select_n.90), dynamic_slice_sizes={1} | dynamic-slice | bytes 12 | tf_op jit(solution)/shard_map/jit(dynamic_index_in_dim)/dynamic_slice | solution.py:156
  13.5 0.6 %pad_maximum_fusion.2.scale = f32[2]{0:T(128)S(1)} fusion(f32[1]{0:T(128)} %bitcast.3, f32[1]{0:T(128)} %dynamic_slice.8), kind=kLoop, calls=%fused_computation.38 | loop fusion | flops 2 | bytes 16 | tf_op jit(solution)/shard_map/stack | solution.py:155
  14.2 1.1 %copy-done.1 = bf16[1,160,2688]{2,1,0:T(8,128)(2,1)S(1)} copy-done((bf16[1,160,2688]{2,1,0:T(8,128)(2,1)S(1)}, bf16[1,160,2688]{2,1,0:T(8,128)(2,1)}, u32[]{:S(2)}) %copy-start.1) | copy-done | bytes 860184
  15.3 1.2 %copy-done.2 = bf16[1,160,2688]{2,1,0:T(8,128)(2,1)S(1)} copy-done((bf16[1,160,2688]{2,1,0:T(8,128)(2,1)S(1)}, bf16[1,160,2688]{2,1,0:T(8,128)(2,1)}, u32[]{:S(2)}) %copy-start.2) | copy-done | bytes 860184
  16.5 1.2 %copy-done.3 = bf16[1,160,2688]{2,1,0:T(8,128)(2,1)S(1)} copy-done((bf16[1,160,2688]{2,1,0:T(8,128)(2,1)S(1)}, bf16[1,160,2688]{2,1,0:T(8,128)(2,1)}, u32[]{:S(2)}) %copy-start.3) | copy-done | bytes 860184
  17.7 1.2 %copy-done.4 = bf16[160,2688]{1,0:T(8,128)(2,1)S(1)} copy-done((bf16[160,2688]{1,0:T(8,128)(2,1)S(1)}, bf16[160,2688]{1,0:T(8,128)(2,1)}, u32[]{:S(2)}) %copy-start.4) | copy-done | bytes 860184
  18.8 13.8 %shard_map.82 = bf16[128,1024]{1,0:T(8,128)(2,1)S(1)} custom-call(f32[2,160]{1,0:T(2,128)S(1)} %pad_maximum_fusion.1.lens, f32[2]{0:T(128)S(1)} %pad_maximum_fusion.2.scale, f32[1,128]{1,0:T(1,128)S(1)} %convert_bitcast_fusion.waves, s32[160,1]{1,0:T(8,128)S(1)} %copy.17.lens_col, bf16[1,160,2688]{2,1,0:T(8,128)(2,1)S(1)} %copy-done.1, ...), custom_call_target="tpu_custom_call" | custom-call | tf_op jit(solution)/shard_map/pallas_call | solution.py:161
  32.6 0.8 %reshape.281 = bf16[32,4,1024]{2,1,0:T(4,128)(2,1)} reshape(bf16[128,1024]{1,0:T(8,128)(2,1)S(1)} %shard_map.82) | data formatting | bytes 524288 | tf_op jit(solution)/shard_map/reshape | solution.py:195
  33.4 4.9 %all-to-all-start = ((bf16[32,4,1024]{2,1,0:T(4,128)(2,1)}), bf16[32,4,1024]{2,1,0:T(4,128)(2,1)S(1)}, u32[]{:S(2)}, u32[]{:S(2)}) async-start(bf16[32,4,1024]{2,1,0:T(4,128)(2,1)} %reshape.281), calls=%async_computation | async-start | bytes 524288 | tf_op jit(solution)/shard_map/all_to_all | solution.py:194
  38.8 10.6 %all-to-all-done = bf16[32,4,1024]{2,1,0:T(4,128)(2,1)S(1)} async-done(((bf16[32,4,1024]{2,1,0:T(4,128)(2,1)}), bf16[32,4,1024]{2,1,0:T(4,128)(2,1)S(1)}, u32[]{:S(2)}, u32[]{:S(2)}) %all-to-all-start) | async-done | bytes 262176 | tf_op jit(solution)/shard_map/all_to_all | solution.py:194
  49.4 0.8 %reshape.288 = f32[8,4,4,3,2,160]{5,4,3,2,1,0:T(2,128)S(1)} reshape(f32[32,4,960]{2,1,0:T(4,128)S(1)} %slice_convert_fusion) | data formatting | bytes 983040 | tf_op jit(solution)/shard_map/reshape | solution.py:198
  50.2 0.4 fusion.13
  50.8 2.3 %fusion.14 = f32[8,4,4,2,160]{4,0,1,3,2:T(8,128)S(1)} fusion(f32[8,4,4,2,160]{4,0,1,3,2:T(8,128)S(1)} %rev.9), kind=kOutput, calls=%fused_computation.42 | output fusion | flops 122880 | bytes 327680 | tf_op jit(solution)/shard_map/jit(cumsum)/reduce_window_sum | solution.py:200
  53.3 0.3 fusion.2
  53.6 0.4 rev.11
  54.2 0.2 maximum_bitcast_fusion
  54.6 0.2 fusion.15
  54.9 0.7 %fusion.9 = bf16[2,2,4,2,256]{4,3,2,1,0:T(2,128)(2,1)} fusion(bf16[2,4,2,4,2,256]{5,4,3,2,1,0:T(2,128)(2,1)S(1)} %reshape.285, pred[2,256]{1,0:T(4,128)(4,1)S(1)} %get-tuple-element.13, pred[2,256]{1,0:T(4,128)(4,1)S(1)} %get-tuple-element.12, pred[2,256]{1,0:T(4,128)(4,1)S(1)} %get-tuple-element.11, pred[2,256]{1,0:T(4,128)(4,1)S(1)} %get-tuple-element.10), kind=kLoop, calls=%fused_computation.22 | loop fusion | flops 32768 | bytes 83968 | tf_op jit(solution)/shard_map/convert_element_type | solution.py:221
  (31 shorter events, 1.5 us)
Async XLA Ops:
  0.0 54.6 %copy-start = (bf16[2,640,256]{2,1,0:T(8,128)(2,1)S(1)}, bf16[2,640,256]{2,1,0:T(8,128)(2,1)}, u32[]{:S(2)}) copy-start(bf16[2,640,256]{2,1,0:T(8,128)(2,1)} %param.15) | copy-start | bytes 1966084
  0.0 0.7 %copy-start.8 = (u32[32]{0:T(128)S(1)}, u32[32]{0:T(128)}, u32[]{:S(2)}) copy-start(u32[32]{0:T(128)} %constant.65) | copy-start | bytes 388
  2.0 0.7 %copy-start.5 = (s32[40]{0:T(128)S(1)}, s32[40]{0:T(128)}, u32[]{:S(2)}) copy-start(s32[40]{0:T(128)} %param.13) | copy-start | bytes 484
  11.6 0.7 %copy-start.7 = (s32[128]{0:T(128)S(1)}, s32[128]{0:T(128)}, u32[]{:S(2)}) copy-start(s32[128]{0:T(128)} %param.14) | copy-start | bytes 1540
  12.3 0.7 %copy-start.6 = (f32[4]{0:T(128)S(1)}, f32[4]{0:T(128)}, u32[]{:S(2)}) copy-start(f32[4]{0:T(128)} %param.12) | copy-start | bytes 52
  14.2 1.2 %copy-start.1 = (bf16[1,160,2688]{2,1,0:T(8,128)(2,1)S(1)}, bf16[1,160,2688]{2,1,0:T(8,128)(2,1)}, u32[]{:S(2)}) copy-start(bf16[1,160,2688]{2,1,0:T(8,128)(2,1)} %u.1) | copy-start | bytes 2580484
  15.3 1.2 %copy-start.2 = (bf16[1,160,2688]{2,1,0:T(8,128)(2,1)S(1)}, bf16[1,160,2688]{2,1,0:T(8,128)(2,1)}, u32[]{:S(2)}) copy-start(bf16[1,160,2688]{2,1,0:T(8,128)(2,1)} %v.1) | copy-start | bytes 2580484
  16.5 1.2 %copy-start.3 = (bf16[1,160,2688]{2,1,0:T(8,128)(2,1)S(1)}, bf16[1,160,2688]{2,1,0:T(8,128)(2,1)}, u32[]{:S(2)}) copy-start(bf16[1,160,2688]{2,1,0:T(8,128)(2,1)} %temp.1) | copy-start | bytes 2580484
  17.7 1.2 %copy-start.4 = (bf16[160,2688]{1,0:T(8,128)(2,1)S(1)}, bf16[160,2688]{1,0:T(8,128)(2,1)}, u32[]{:S(2)}) copy-start(bf16[160,2688]{1,0:T(8,128)(2,1)} %oro.1) | copy-start | bytes 2580484
  33.4 15.9 %all-to-all-start = ((bf16[32,4,1024]{2,1,0:T(4,128)(2,1)}), bf16[32,4,1024]{2,1,0:T(4,128)(2,1)S(1)}, u32[]{:S(2)}, u32[]{:S(2)}) async-start(bf16[32,4,1024]{2,1,0:T(4,128)(2,1)} %reshape.281), calls=%async_computation | async-start | bytes 524288 | tf_op jit(solution)/shard_map/all_to_all | solution.py:194

commit v2 on v1

--- a/solution.py
+++ b/solution.py
@@ -31,14 +31,95 @@
     return a[0] * b[0] - a[1] * b[1], a[0] * b[1] + a[1] * b[0]
 
 
-def transform(high, high_pad, lens, scale, waves, lens_col, u, v, temp, oro, out, spread, sums, gathered):
+MESH = pl.DeviceIdType.MESH
+
+
+def swap(axes, x, out, landed, send_sem, recv_sem):
+    sizes = [lax.axis_size(a) for a in axes]
+    count = 1
+    me = 0
+    for a, size in zip(axes, sizes):
+        count = count * size
+        me = me * size + lax.axis_index(a)
+    shared = x.shape[0] != count
+
+    def device(turn):
+        peer = lax.rem(me + turn, count)
+        if len(axes) == 1:
+            return peer, {axes[0]: peer}
+        return peer, {axes[0]: lax.div(peer, sizes[1]), axes[1]: lax.rem(peer, sizes[1])}
+
+    barrier = pltpu.get_barrier_semaphore()
+
+    def greet(turn, carry):
+        pl.semaphore_signal(barrier, inc=1, device_id=device(turn)[1], device_id_type=MESH)
+        return carry
+
+    lax.fori_loop(1, count, greet, 0)
+    pl.semaphore_wait(barrier, count - 1)
+
+    def copy(turn):
+        peer, where = device(turn)
+        return pltpu.make_async_remote_copy(
+            src_ref=x.at[0 if shared else peer],
+            dst_ref=landed.at[me],
+            send_sem=send_sem.at[turn],
+            recv_sem=recv_sem.at[turn],
+            device_id=where,
+            device_id_type=MESH,
+        )
+
+    def begin(turn, carry):
+        copy(turn).start()
+        return carry
+
+    def finish(turn, carry):
+        copy(turn).wait()
+        return carry
+
+    lax.fori_loop(1, count, begin, 0)
+    landed[me] = x[0 if shared else me]
+    lax.fori_loop(1, count, finish, 0)
+    out[...] = landed[...]
+
+
+def exchange(x, axes, count, number):
+    shape = (count,) + x.shape[1:]
+    vmem = pl.BlockSpec(memory_space=pltpu.VMEM)
+    return pl.pallas_call(
+        functools.partial(swap, axes),
+        out_shape=jax.ShapeDtypeStruct(shape, x.dtype),
+        in_specs=[vmem],
+        out_specs=vmem,
+        scratch_shapes=[
+            pltpu.VMEM(shape, x.dtype),
+            pltpu.SemaphoreType.DMA((count,)),
+            pltpu.SemaphoreType.DMA((count,)),
+        ],
+        compiler_params=pltpu.CompilerParams(
+            collective_id=number, has_side_effects=True, vmem_limit_bytes=24 * 2**20
+        ),
+    )(x)
+
+
+def transform(high, high_pad, lens, depths, waves, u, v, temp, oro, out, spread, sums, gathered):
     step = pl.program_id(0)
     steps = pl.num_programs(0)
     rows = steps * STRIP
     south = lax.axis_index("wide") * 2 >= lax.axis_size("wide")
-    depth = scale[0]
-    ground = scale[1]
-    limit = jnp.broadcast_to(lens_col[...], (STRIP, LANES))
+    level = lax.axis_index("lev")
+    depth = depths[level]
+    ground = jnp.where(level == lax.axis_size("lev") - 1, 1.0, 0.0)
+    share = rows // lens.shape[0]
+
+    def row_length(r):
+        row = step * STRIP + r
+        return lens[lax.div(row, share), 0, lax.rem(row, share)]
+
+    backward = lax.broadcasted_iota(jnp.int32, (STRIP, LANES), 0)
+    limit = jnp.zeros((STRIP, LANES), jnp.int32)
+    for r in range(STRIP):
+        limit = jnp.where(backward == r, row_length(r), limit)
     lane = lax.broadcasted_iota(jnp.int32, (STRIP, LANES), 1)
     for h in range(high_pad):
         at = pl.ds(h * STRIP, STRIP)
@@ -63,8 +144,8 @@
         m = jnp.broadcast_to(waves[:, chunk * LANES:(chunk + 1) * LANES], (8, LANES))
 
         def one_row(r, carry):
-            length = lens[0, step * STRIP + r]
-            inverse = lens[1, step * STRIP + r]
+            length = jnp.broadcast_to(row_length(r).astype(jnp.float32), (8, LANES))
+            inverse = 1.0 / length
             data = jnp.concatenate(
                 [spread[c, pl.ds(r, high_pad, stride=STRIP), :] for c in range(3)], axis=0
             ).astype(jnp.bfloat16)
@@ -104,17 +185,13 @@
         lax.fori_loop(0, STRIP, one_row, 0, unroll=4)
 
         block = jnp.where(south, steps - 1 - step, step) * STRIP
-        lens_here = jnp.broadcast_to(lens_col[...], (STRIP, LANES)).astype(jnp.float32)
-        backward = lax.broadcasted_iota(jnp.int32, (STRIP, LANES), 0)
         m16 = jnp.broadcast_to(waves[:, chunk * LANES:(chunk + 1) * LANES], (STRIP, LANES))
-        factor = jnp.zeros((STRIP, LANES), jnp.float32)
+        length = jnp.zeros((STRIP, LANES), jnp.int32)
         for r in range(STRIP):
-            length = lens[0, step * STRIP + r]
-            inverse = lens[1, step * STRIP + r]
             place = jnp.where(south, STRIP - 1 - r, r)
-            factor = jnp.where(
-                backward == place, jnp.where(2.0 * m16 < length, inverse, 0.0), factor
-            )
+            length = jnp.where(backward == place, row_length(r), length)
+        length = length.astype(jnp.float32)
+        factor = jnp.where(2.0 * m16 < length, 1.0 / length, 0.0)
         for k in range(6):
             total = sums[k, pl.ds(0, STRIP, stride=8), :]
             for s in range(1, 8):
@@ -150,11 +227,9 @@
     high_pad = -(-high // 8) * 8
     steps = rows // STRIP
     packed = -(-6 * rows // LANES) * LANES
-    band = lax.all_gather(lens, "lev", tiled=True)
-    band_float = band.astype(jnp.float32)
-    scale = jnp.stack(
-        [lax.dynamic_index_in_dim(depths, lev, 0, False), (lev == lev_count - 1).astype(jnp.float32)]
-    )
+    wide_held = -(-lens.shape[0] // LANES) * LANES
+    held = jnp.pad(lens, (0, wide_held - lens.shape[0])).reshape(1, 1, wide_held)
+    band = exchange(held, ("lev",), lev_count, 1)
     smem = pl.BlockSpec(memory_space=pltpu.SMEM)
     field = pl.BlockSpec((STRIP, samples), lambda i: (i, 0))
     field3 = pl.BlockSpec((None, STRIP, samples), lambda i: (0, i, 0))
@@ -166,7 +241,6 @@
             smem,
             smem,
             pl.BlockSpec((1, waves_total), lambda i: (0, 0)),
-            pl.BlockSpec((STRIP, 1), lambda i: (i, 0)),
             field3,
             field3,
             field3,
@@ -178,12 +252,11 @@
             pltpu.VMEM((6, STRIP * 8, LANES), jnp.float32),
             pltpu.VMEM((waves_total // LANES, packed, LANES), jnp.float32),
         ],
-        compiler_params=pltpu.CompilerParams(vmem_limit_bytes=40 * 2**20),
+        compiler_params=pltpu.CompilerParams(vmem_limit_bytes=60 * 2**20),
     )(
-        jnp.stack([band_float, 1.0 / band_float]),
-        scale,
+        band,
+        depths,
         orders.astype(jnp.float32)[None],
-        band[:, None],
         u,
         v,
         temp,
@@ -191,9 +264,7 @@
     )
     devices = lev_count * wide_count
     slots = waves_total // devices
-    got = lax.all_to_all(
-        coefs.reshape(devices, slots, packed), ("wide", "lev"), split_axis=0, concat_axis=0, tiled=True
-    )
+    got = exchange(coefs.reshape(devices, slots, packed), ("wide", "lev"), devices, 0)
     got = got[:, :, :6 * rows].astype(jnp.float32)
     got = got.reshape(wide_count, lev_count, slots, 3, 2, rows)
     under = got[:, :, :, 1]

time: 55.9 us -> 40 us (0.72)
  Pallas kernels: 13.8 us -> 32.7 us
  waiting for transfers between devices: 10.6 us -> 0 us
  blocking collectives: 8.82 us -> 0 us
  local copies, waits for them, and re-layouts: 11.8 us -> 4.05 us
  starting transfers between devices: 4.92 us -> 0 us
  other arithmetic: 4.52 us -> 2.65 us
  between operations: 0.86 us -> 0.16 us
    pallas_call x0 -> x2, Pallas kernels: none -> 17 us  [exchange(): pl.pallas_call(functools.partial(swap, axes), out_shape=jax.ShapeDtypeStr...]
    all_to_all x1 -> x0, waiting for transfers between devices: 10.6 us -> none  [local(): lax.all_to_all(coefs.reshape(devices, slots, packed), ('wide', 'lev'), sp...]
    unnamed x1 -> x0, blocking collectives: 8.82 us -> none
    unnamed x23 -> x6, local copies, waits for them, and re-layouts: 8.27 us -> 0.58 us
    all_to_all x1 -> x0, starting transfers between devices: 4.92 us -> none  [local(): lax.all_to_all(coefs.reshape(devices, slots, packed), ('wide', 'lev'), sp...]
    another operation x1, other arithmetic: 2.27 us -> 0.09 us  [local(): below = jnp.cumsum(under[:, ::-1], axis=1)[:, ::-1] - under]
    pallas_call x1, Pallas kernels: 13.8 us -> 15.7 us  [local(): pl.pallas_call(functools.partial(transform, high, high_pad), grid=(steps,...]
    reshape x0 -> x1, local copies, waits for them, and re-layouts: none -> 0.72 us  [local(): jnp.pad(lens, (0, wide_held - lens.shape[0])).reshape(1, 1, wide_held)]
  transfers between devices with their start and end apart: 1 -> 0, of which waited for: 1 -> 0; matrix products, arithmetic and copies ran while one was open for 1% -> 0% of each run, Pallas kernels for 0% -> 0%
where the time goes in v2:
time: 40 us; the launch traced here: 39.8 us
  Pallas kernels  32.7 us (82%)
  local copies, waits for them, and re-layouts  4.05 us (10%)
  other arithmetic  2.65 us (7%)
    pallas_call x2, Pallas kernels, exchange(): pl.pallas_call(functools.partial(swap, axes), out_shape=jax.ShapeDtypeStr...  17 us
    pallas_call x1, Pallas kernels, local(): pl.pallas_call(functools.partial(transform, high, high_pad), grid=(steps,...  15.7 us
    reshape x1, local copies, waits for them, and re-layouts, local(): coefs.reshape(devices, slots, packed)  1.05 us
    reshape x1, local copies, waits for them, and re-layouts, local(): got = got.reshape(wide_count, lev_count, slots, 3, 2, rows)  0.82 us

profile of v2, /device:TPU:0, one launch (start us, length us, event | category | flops | bytes accessed | tf_op | source)
XLA Modules:
  0.0 39.8 jit_solution(12569654526299390132)
XLA Ops:
  0.0 0.7 %pad_bitcast_fusion.x = s32[1,1,128]{2,1,0:T(1,128)S(1)} fusion(s32[40]{0:T(128)} %param.13), kind=kLoop, calls=%fused_computation.38 | loop fusion | bytes 672 | tf_op jit(solution)/shard_map/reshape | solution.py:231
  0.7 6.0 %shard_map.82.lens = s32[4,1,128]{2,1,0:T(1,128)S(1)} custom-call(s32[1,1,128]{2,1,0:T(1,128)S(1)} %pad_bitcast_fusion.x), custom_call_target="tpu_custom_call" | custom-call | tf_op jit(solution)/shard_map/pallas_call | solution.py:89
  6.8 0.6 %copy-done.1 = s32[4,1,128]{2,1,0:T(1,128)} copy-done((s32[4,1,128]{2,1,0:T(1,128)}, s32[4,1,128]{2,1,0:T(1,128)S(1)}, u32[]{:S(2)}) %copy-start.1) | copy-done | bytes 2072
  7.4 0.5 %convert_bitcast_fusion.waves = f32[1,128]{1,0:T(1,128)} fusion(s32[128]{0:T(128)S(1)} %copy-done.2), kind=kLoop, calls=%fused_computation.37 | loop fusion | flops 128 | bytes 1024 | tf_op jit(solution)/shard_map/broadcast_in_dim | solution.py:259
  7.9 15.7 %shard_map.83 = bf16[128,1024]{1,0:T(8,128)(2,1)} custom-call(s32[4,1,128]{2,1,0:T(1,128)} %copy-done.1, f32[4]{0:T(128)} %depths.1, f32[1,128]{1,0:T(1,128)} %convert_bitcast_fusion.waves, bf16[1,160,2688]{2,1,0:T(8,128)(2,1)} %u.1, bf16[1,160,2688]{2,1,0:T(8,128)(2,1)} %v.1, bf16[1,160,2688]{2,1,0:T(8,128)(2,1)} %temp.1, bf16[160,2688]{1,0:T(8,128)(2,1)} %oro.1), custom_call_target="tpu_custom_call" | custom-call | tf_op jit(solution)/shard_map/pallas_call | solution.py:236
  23.6 1.1 %reshape.285.x = bf16[32,4,1024]{2,1,0:T(4,128)(2,1)S(1)} reshape(bf16[128,1024]{1,0:T(8,128)(2,1)} %shard_map.83) | data formatting | bytes 524288 | tf_op jit(solution)/shard_map/reshape | solution.py:267
  24.6 10.9 %shard_map.84 = bf16[32,4,1024]{2,1,0:T(4,128)(2,1)S(1)} custom-call(bf16[32,4,1024]{2,1,0:T(4,128)(2,1)S(1)} %reshape.285.x), custom_call_target="tpu_custom_call" | custom-call | tf_op jit(solution)/shard_map/pallas_call | solution.py:89
  35.6 0.1 slice_convert_fusion
  35.7 0.8 %reshape.291 = f32[8,4,4,3,2,160]{5,4,3,2,1,0:T(2,128)S(1)} reshape(f32[32,4,960]{2,1,0:T(4,128)S(1)} %slice_convert_fusion) | data formatting | bytes 983040 | tf_op jit(solution)/shard_map/reshape | solution.py:269
  36.5 0.3 slice_bitcast_fusion
  36.8 0.1 fusion.14
  36.9 0.2 fusion.2
  37.1 0.1 pad_maximum_fusion
  37.2 0.2 fusion.3
  37.4 0.1 fusion.4
  37.6 0.4 %maximum_bitcast_fusion = bf16[4,2,2,4,2,4,160]{6,2,4,0,3,5,1:T(2,128)(2,1)S(1)} fusion(bf16[1,4,4,4,2,2,160]{6,5,4,3,2,1,0:T(2,128)(2,1)S(1)} %fusion.4, bf16[1,4,4,4,2,2,160]{6,5,4,3,2,1,0:T(2,128)(2,1)S(1)} %get-tuple-element.5), kind=kLoop, calls=%fused_computation.8 | loop fusion | flops 81920 | bytes 327680 | tf_op jit(solution)/shard_map/transpose | solution.py:277
  38.0 0.2 copy.18
  38.2 0.2 reshape.288
  38.4 0.2 fusion.15
  38.7 0.1 dynamic_slice.3
  38.8 0.1 reshape.283
  38.9 0.1 subtract_reduce_fusion
  39.0 0.1 broadcast_compare_fusion
  39.1 0.7 %fusion.9 = bf16[2,2,4,2,256]{4,3,2,1,0:T(2,128)(2,1)} fusion(bf16[2,4,2,4,2,256]{5,4,3,2,1,0:T(2,128)(2,1)S(1)} %reshape.289, pred[2,256]{1,0:T(4,128)(4,1)S(1)} %get-tuple-element.12, pred[2,256]{1,0:T(4,128)(4,1)S(1)} %get-tuple-element.11, pred[2,256]{1,0:T(4,128)(4,1)S(1)} %get-tuple-element.10, pred[2,256]{1,0:T(4,128)(4,1)S(1)} %get-tuple-element.9), kind=kLoop, calls=%fused_computation.22 | loop fusion | flops 32768 | bytes 83968 | tf_op jit(solution)/shard_map/convert_element_type | solution.py:292
  (9 shorter events, 0.1 us)
Async XLA Ops:
  0.0 38.4 %copy-start = (bf16[2,640,256]{2,1,0:T(8,128)(2,1)S(1)}, bf16[2,640,256]{2,1,0:T(8,128)(2,1)}, u32[]{:S(2)}) copy-start(bf16[2,640,256]{2,1,0:T(8,128)(2,1)} %param.15) | copy-start | bytes 1966084
  0.7 6.6 %copy-start.2 = (s32[128]{0:T(128)S(1)}, s32[128]{0:T(128)}, u32[]{:S(2)}) copy-start(s32[128]{0:T(128)} %param.14) | copy-start | bytes 1540
  6.8 0.6 %copy-start.1 = (s32[4,1,128]{2,1,0:T(1,128)}, s32[4,1,128]{2,1,0:T(1,128)S(1)}, u32[]{:S(2)}) copy-start(s32[4,1,128]{2,1,0:T(1,128)S(1)} %shard_map.82.lens) | copy-start | bytes 6148

commit v3 on v2

--- a/solution.py
+++ b/solution.py
@@ -141,7 +141,7 @@
     sub = lax.broadcasted_iota(jnp.int32, (8, LANES), 0).astype(jnp.float32)
     chunks = waves.shape[1] // LANES
     for chunk in range(chunks):
-        m = jnp.broadcast_to(waves[:, chunk * LANES:(chunk + 1) * LANES], (8, LANES))
+        m = jnp.broadcast_to(waves[:, chunk * LANES:(chunk + 1) * LANES], (8, LANES)).astype(jnp.float32)
 
         def one_row(r, carry):
             length = jnp.broadcast_to(row_length(r).astype(jnp.float32), (8, LANES))
@@ -162,10 +162,10 @@
                 axis=1,
             ).astype(jnp.bfloat16)
             part = jnp.dot(data, table, preferred_element_type=jnp.float32)
-            outer = [
-                unit(m * (sub * float(LANES) + float(8 * LANES * g)), length, inverse)
-                for g in range(high_pad // 8)
-            ]
+            outer = [unit(m * (sub * float(LANES)), length, inverse)]
+            stride = unit(m * float(8 * LANES), length, inverse)
+            while len(outer) < high_pad // 8:
+                outer.append(times(outer[-1], stride))
             place = jnp.where(south, STRIP - 1 - r, r)
             for c in range(3):
                 real = jnp.zeros((8, LANES), jnp.float32)
@@ -182,10 +182,12 @@
                 sums[2 * c + 1, at, :] = imag
             return carry
 
-        lax.fori_loop(0, STRIP, one_row, 0, unroll=4)
+        lax.fori_loop(0, STRIP, one_row, 0, unroll=8)
 
         block = jnp.where(south, steps - 1 - step, step) * STRIP
-        m16 = jnp.broadcast_to(waves[:, chunk * LANES:(chunk + 1) * LANES], (STRIP, LANES))
+        m16 = jnp.broadcast_to(
+            waves[:, chunk * LANES:(chunk + 1) * LANES], (STRIP, LANES)
+        ).astype(jnp.float32)
         length = jnp.zeros((STRIP, LANES), jnp.int32)
         for r in range(STRIP):
             place = jnp.where(south, STRIP - 1 - r, r)
@@ -210,8 +212,11 @@
     def _():
         for chunk in range(chunks):
             for b in range(gathered.shape[1] // LANES):
-                out[chunk * LANES:(chunk + 1) * LANES, b * LANES:(b + 1) * LANES] = (
-                    gathered[chunk, b * LANES:(b + 1) * LANES, :].T.astype(out.dtype)
+                turned = gathered[chunk, b * LANES:(b + 1) * LANES, :].T.astype(out.dtype)
+                slots = out.shape[1]
+                owners = LANES // slots
+                out[chunk * owners:(chunk + 1) * owners, :, b * LANES:(b + 1) * LANES] = (
+                    turned.reshape(owners, slots, LANES)
                 )
 
 
@@ -226,9 +231,10 @@
     high = samples // LANES
     high_pad = -(-high // 8) * 8
     steps = rows // STRIP
+    devices = lev_count * wide_count
+    slots = waves_total // devices
     packed = -(-6 * rows // LANES) * LANES
-    wide_held = -(-lens.shape[0] // LANES) * LANES
-    held = jnp.pad(lens, (0, wide_held - lens.shape[0])).reshape(1, 1, wide_held)
+    held = lens.reshape(1, 1, lens.shape[0])
     band = exchange(held, ("lev",), lev_count, 1)
     smem = pl.BlockSpec(memory_space=pltpu.SMEM)
     field = pl.BlockSpec((STRIP, samples), lambda i: (i, 0))
@@ -236,7 +242,7 @@
     coefs = pl.pallas_call(
         functools.partial(transform, high, high_pad),
         grid=(steps,),
-        out_shape=jax.ShapeDtypeStruct((waves_total, packed), jnp.bfloat16),
+        out_shape=jax.ShapeDtypeStruct((devices, slots, packed), jnp.bfloat16),
         in_specs=[
             smem,
             smem,
@@ -246,7 +252,7 @@
             field3,
             field,
         ],
-        out_specs=pl.BlockSpec((waves_total, packed), lambda i: (0, 0)),
+        out_specs=pl.BlockSpec((devices, slots, packed), lambda i: (0, 0, 0)),
         scratch_shapes=[
             pltpu.VMEM((3, high_pad * STRIP, LANES), jnp.float32),
             pltpu.VMEM((6, STRIP * 8, LANES), jnp.float32),
@@ -256,15 +262,13 @@
     )(
         band,
         depths,
-        orders.astype(jnp.float32)[None],
+        orders[None],
         u,
         v,
         temp,
         oro,
     )
-    devices = lev_count * wide_count
-    slots = waves_total // devices
-    got = exchange(coefs.reshape(devices, slots, packed), ("wide", "lev"), devices, 0)
+    got = exchange(coefs, ("wide", "lev"), devices, 0)
     got = got[:, :, :6 * rows].astype(jnp.float32)
     got = got.reshape(wide_count, lev_count, slots, 3, 2, rows)
     under = got[:, :, :, 1]

time: 40 us -> 37.4 us (0.935)
  Pallas kernels: 32.7 us -> 30.1 us
  local copies, waits for them, and re-layouts: 4.05 us -> 4.59 us
  other arithmetic: 2.65 us -> 2.15 us
    pallas_call x1, Pallas kernels: 15.7 us -> 13.2 us  [local(): pl.pallas_call(functools.partial(transform, high, high_pad), grid=(steps,...]
    unnamed x6 -> x10, local copies, waits for them, and re-layouts: 0.58 us -> 2.9 us
    reshape x2 -> x0, local copies, waits for them, and re-layouts: 1.78 us -> none  [the longest x1 1.05 us: local(): coefs.reshape(devices, slots, packed)]
    broadcast_in_dim x1 -> x0, other arithmetic: 0.53 us -> none  [local(): orders.astype(jnp.float32)[None]]
where the time goes in v3:
time: 37.4 us; the launch traced here: 37.2 us
  Pallas kernels  30.1 us (80%)
  local copies, waits for them, and re-layouts  4.59 us (12%)
  other arithmetic  2.15 us (6%)
    pallas_call x2, Pallas kernels, exchange(): pl.pallas_call(functools.partial(swap, axes), out_shape=jax.ShapeDtypeStr...  16.8 us
    pallas_call x1, Pallas kernels, local(): pl.pallas_call(functools.partial(transform, high, high_pad), grid=(steps,...  13.2 us
    unnamed x10, local copies, waits for them, and re-layouts  2.9 us
    reshape x1, local copies, waits for them, and re-layouts, local(): got = got.reshape(wide_count, lev_count, slots, 3, 2, rows)  0.82 us

profile of v3, /device:TPU:0, one launch (start us, length us, event | category | flops | bytes accessed | tf_op | source)
XLA Modules:
  0.0 37.2 jit_solution(950346325124571669)
XLA Ops:
  0.0 0.7 %copy-done.3 = s32[40]{0:T(128)S(1)} copy-done((s32[40]{0:T(128)S(1)}, s32[40]{0:T(128)}, u32[]{:S(2)}) %copy-start.3) | copy-done | bytes 184
  0.7 6.0 %shard_map.82.lens = s32[4,1,40]{2,1,0:T(1,128)S(1)} custom-call(s32[1,1,40]{2,1,0:T(1,128)S(1)} %bitcast.65), custom_call_target="tpu_custom_call" | custom-call | tf_op jit(solution)/shard_map/pallas_call | solution.py:89
  6.8 0.6 %copy-done.2 = s32[4,1,40]{2,1,0:T(1,128)} copy-done((s32[4,1,40]{2,1,0:T(1,128)}, s32[4,1,40]{2,1,0:T(1,128)S(1)}, u32[]{:S(2)}) %copy-start.2) | copy-done | bytes 664
  7.4 13.2 %shard_map.83.x = bf16[32,4,1024]{2,1,0:T(4,128)(2,1)} custom-call(s32[4,1,40]{2,1,0:T(1,128)} %copy-done.2, f32[4]{0:T(128)} %depths.1, s32[1,128]{1,0:T(1,128)} %bitcast.66, bf16[1,160,2688]{2,1,0:T(8,128)(2,1)} %u.1, bf16[1,160,2688]{2,1,0:T(8,128)(2,1)} %v.1, bf16[1,160,2688]{2,1,0:T(8,128)(2,1)} %temp.1, bf16[160,2688]{1,0:T(8,128)(2,1)} %oro.1), custom_call_target="tpu_custom_call" | custom-call | tf_op jit(solution)/shard_map/pallas_call | solution.py:242
  20.6 0.9 %copy-done.1 = bf16[32,4,1024]{2,1,0:T(4,128)(2,1)S(1)} copy-done((bf16[32,4,1024]{2,1,0:T(4,128)(2,1)S(1)}, bf16[32,4,1024]{2,1,0:T(4,128)(2,1)}, u32[]{:S(2)}) %copy-start.1) | copy-done | bytes 262168
  21.5 10.8 %shard_map.84 = bf16[32,4,1024]{2,1,0:T(4,128)(2,1)S(1)} custom-call(bf16[32,4,1024]{2,1,0:T(4,128)(2,1)S(1)} %copy-done.1), custom_call_target="tpu_custom_call" | custom-call | tf_op jit(solution)/shard_map/pallas_call | solution.py:89
  32.3 0.1 slice_convert_fusion
  32.4 0.8 %reshape.287 = f32[8,4,4,3,2,160]{5,4,3,2,1,0:T(2,128)S(1)} reshape(f32[32,4,960]{2,1,0:T(4,128)S(1)} %slice_convert_fusion) | data formatting | bytes 983040 | tf_op jit(solution)/shard_map/reshape | solution.py:273
  33.2 0.3 slice_bitcast_fusion
  33.5 0.1 fusion.14
  33.6 0.2 fusion.2
  33.8 0.1 pad_maximum_fusion
  34.0 0.2 fusion.3
  34.2 0.2 fusion.4
  34.4 0.4 %maximum_bitcast_fusion = bf16[4,2,2,4,2,4,160]{6,2,4,0,3,5,1:T(2,128)(2,1)S(1)} fusion(bf16[1,4,4,4,2,2,160]{6,5,4,3,2,1,0:T(2,128)(2,1)S(1)} %fusion.4, bf16[1,4,4,4,2,2,160]{6,5,4,3,2,1,0:T(2,128)(2,1)S(1)} %get-tuple-element.5), kind=kLoop, calls=%fused_computation.8 | loop fusion | flops 81920 | bytes 327680 | tf_op jit(solution)/shard_map/transpose | solution.py:281
  34.8 0.2 copy.18
  35.0 0.2 reshape.284
  35.2 0.2 fusion.15
  35.5 0.6 %copy-done.4 = s32[128]{0:T(128)S(1)} copy-done((s32[128]{0:T(128)S(1)}, s32[128]{0:T(128)}, u32[]{:S(2)}) %copy-start.4) | copy-done | bytes 536
  36.2 0.1 dynamic_slice.3
  36.2 0.1 reshape.280
  36.3 0.1 subtract_reduce_fusion
  36.4 0.1 broadcast_compare_fusion
  36.5 0.7 %fusion.9 = bf16[2,2,4,2,256]{4,3,2,1,0:T(2,128)(2,1)} fusion(bf16[2,4,2,4,2,256]{5,4,3,2,1,0:T(2,128)(2,1)S(1)} %reshape.285, pred[2,256]{1,0:T(4,128)(4,1)S(1)} %get-tuple-element.12, pred[2,256]{1,0:T(4,128)(4,1)S(1)} %get-tuple-element.11, pred[2,256]{1,0:T(4,128)(4,1)S(1)} %get-tuple-element.10, pred[2,256]{1,0:T(4,128)(4,1)S(1)} %get-tuple-element.9), kind=kLoop, calls=%fused_computation.22 | loop fusion | flops 32768 | bytes 83968 | tf_op jit(solution)/shard_map/convert_element_type | solution.py:296
  (10 shorter events, 0.1 us)
Async XLA Ops:
  0.0 35.2 %copy-start = (bf16[2,640,256]{2,1,0:T(8,128)(2,1)S(1)}, bf16[2,640,256]{2,1,0:T(8,128)(2,1)}, u32[]{:S(2)}) copy-start(bf16[2,640,256]{2,1,0:T(8,128)(2,1)} %param.15) | copy-start | bytes 1966084
  0.0 0.7 %copy-start.3 = (s32[40]{0:T(128)S(1)}, s32[40]{0:T(128)}, u32[]{:S(2)}) copy-start(s32[40]{0:T(128)} %param.13) | copy-start | bytes 484
  6.8 0.6 %copy-start.2 = (s32[4,1,40]{2,1,0:T(1,128)}, s32[4,1,40]{2,1,0:T(1,128)S(1)}, u32[]{:S(2)}) copy-start(s32[4,1,40]{2,1,0:T(1,128)S(1)} %shard_map.82.lens) | copy-start | bytes 1924
  20.6 0.9 %copy-start.1 = (bf16[32,4,1024]{2,1,0:T(4,128)(2,1)S(1)}, bf16[32,4,1024]{2,1,0:T(4,128)(2,1)}, u32[]{:S(2)}) copy-start(bf16[32,4,1024]{2,1,0:T(4,128)(2,1)} %shard_map.83.x) | copy-start | bytes 786436
  35.5 0.7 %copy-start.4 = (s32[128]{0:T(128)S(1)}, s32[128]{0:T(128)}, u32[]{:S(2)}) copy-start(s32[128]{0:T(128)} %param.14) | copy-start | bytes 1540

commit v4 on v3

--- a/solution.py
+++ b/solution.py
@@ -182,7 +182,7 @@
                 sums[2 * c + 1, at, :] = imag
             return carry
 
-        lax.fori_loop(0, STRIP, one_row, 0, unroll=8)
+        lax.fori_loop(0, STRIP, one_row, 0, unroll=16)
 
         block = jnp.where(south, steps - 1 - step, step) * STRIP
         m16 = jnp.broadcast_to(

time: 37.4 us -> 37.5 us (level)
  no operation moved by 1% of the time
where the time goes in v4:
time: 37.5 us; the launch traced here: 37.3 us
  Pallas kernels  30.2 us (81%)
  local copies, waits for them, and re-layouts  4.59 us (12%)
  other arithmetic  2.15 us (6%)
    pallas_call x2, Pallas kernels, exchange(): pl.pallas_call(functools.partial(swap, axes), out_shape=jax.ShapeDtypeStr...  16.8 us
    pallas_call x1, Pallas kernels, local(): pl.pallas_call(functools.partial(transform, high, high_pad), grid=(steps,...  13.3 us
    unnamed x10, local copies, waits for them, and re-layouts  2.9 us
    reshape x1, local copies, waits for them, and re-layouts, local(): got = got.reshape(wide_count, lev_count, slots, 3, 2, rows)  0.82 us

profile of v4, /device:TPU:0, one launch (start us, length us, event | category | flops | bytes accessed | tf_op | source)
XLA Modules:
  0.0 37.3 jit_solution(16171813841905204916)
XLA Ops:
  0.0 0.7 %copy-done.3 = s32[40]{0:T(128)S(1)} copy-done((s32[40]{0:T(128)S(1)}, s32[40]{0:T(128)}, u32[]{:S(2)}) %copy-start.3) | copy-done | bytes 184
  0.7 6.0 %shard_map.82.lens = s32[4,1,40]{2,1,0:T(1,128)S(1)} custom-call(s32[1,1,40]{2,1,0:T(1,128)S(1)} %bitcast.65), custom_call_target="tpu_custom_call" | custom-call | tf_op jit(solution)/shard_map/pallas_call | solution.py:89
  6.8 0.6 %copy-done.2 = s32[4,1,40]{2,1,0:T(1,128)} copy-done((s32[4,1,40]{2,1,0:T(1,128)}, s32[4,1,40]{2,1,0:T(1,128)S(1)}, u32[]{:S(2)}) %copy-start.2) | copy-done | bytes 664
  7.4 13.3 %shard_map.83.x = bf16[32,4,1024]{2,1,0:T(4,128)(2,1)} custom-call(s32[4,1,40]{2,1,0:T(1,128)} %copy-done.2, f32[4]{0:T(128)} %depths.1, s32[1,128]{1,0:T(1,128)} %bitcast.66, bf16[1,160,2688]{2,1,0:T(8,128)(2,1)} %u.1, bf16[1,160,2688]{2,1,0:T(8,128)(2,1)} %v.1, bf16[1,160,2688]{2,1,0:T(8,128)(2,1)} %temp.1, bf16[160,2688]{1,0:T(8,128)(2,1)} %oro.1), custom_call_target="tpu_custom_call" | custom-call | tf_op jit(solution)/shard_map/pallas_call | solution.py:242
  20.7 0.9 %copy-done.1 = bf16[32,4,1024]{2,1,0:T(4,128)(2,1)S(1)} copy-done((bf16[32,4,1024]{2,1,0:T(4,128)(2,1)S(1)}, bf16[32,4,1024]{2,1,0:T(4,128)(2,1)}, u32[]{:S(2)}) %copy-start.1) | copy-done | bytes 262168
  21.7 10.8 %shard_map.84 = bf16[32,4,1024]{2,1,0:T(4,128)(2,1)S(1)} custom-call(bf16[32,4,1024]{2,1,0:T(4,128)(2,1)S(1)} %copy-done.1), custom_call_target="tpu_custom_call" | custom-call | tf_op jit(solution)/shard_map/pallas_call | solution.py:89
  32.5 0.1 slice_convert_fusion
  32.5 0.8 %reshape.287 = f32[8,4,4,3,2,160]{5,4,3,2,1,0:T(2,128)S(1)} reshape(f32[32,4,960]{2,1,0:T(4,128)S(1)} %slice_convert_fusion) | data formatting | bytes 983040 | tf_op jit(solution)/shard_map/reshape | solution.py:273
  33.3 0.3 slice_bitcast_fusion
  33.6 0.1 fusion.14
  33.7 0.2 fusion.2
  33.9 0.1 pad_maximum_fusion
  34.1 0.2 fusion.3
  34.3 0.2 fusion.4
  34.5 0.4 %maximum_bitcast_fusion = bf16[4,2,2,4,2,4,160]{6,2,4,0,3,5,1:T(2,128)(2,1)S(1)} fusion(bf16[1,4,4,4,2,2,160]{6,5,4,3,2,1,0:T(2,128)(2,1)S(1)} %fusion.4, bf16[1,4,4,4,2,2,160]{6,5,4,3,2,1,0:T(2,128)(2,1)S(1)} %get-tuple-element.5), kind=kLoop, calls=%fused_computation.8 | loop fusion | flops 81920 | bytes 327680 | tf_op jit(solution)/shard_map/transpose | solution.py:281
  34.9 0.2 copy.18
  35.1 0.2 reshape.284
  35.3 0.2 fusion.15
  35.6 0.6 %copy-done.4 = s32[128]{0:T(128)S(1)} copy-done((s32[128]{0:T(128)S(1)}, s32[128]{0:T(128)}, u32[]{:S(2)}) %copy-start.4) | copy-done | bytes 536
  36.3 0.1 dynamic_slice.3
  36.4 0.1 reshape.280
  36.4 0.1 subtract_reduce_fusion
  36.6 0.1 broadcast_compare_fusion
  36.7 0.7 %fusion.9 = bf16[2,2,4,2,256]{4,3,2,1,0:T(2,128)(2,1)} fusion(bf16[2,4,2,4,2,256]{5,4,3,2,1,0:T(2,128)(2,1)S(1)} %reshape.285, pred[2,256]{1,0:T(4,128)(4,1)S(1)} %get-tuple-element.12, pred[2,256]{1,0:T(4,128)(4,1)S(1)} %get-tuple-element.11, pred[2,256]{1,0:T(4,128)(4,1)S(1)} %get-tuple-element.10, pred[2,256]{1,0:T(4,128)(4,1)S(1)} %get-tuple-element.9), kind=kLoop, calls=%fused_computation.22 | loop fusion | flops 32768 | bytes 83968 | tf_op jit(solution)/shard_map/convert_element_type | solution.py:296
  (10 shorter events, 0.1 us)
Async XLA Ops:
  0.0 35.3 %copy-start = (bf16[2,640,256]{2,1,0:T(8,128)(2,1)S(1)}, bf16[2,640,256]{2,1,0:T(8,128)(2,1)}, u32[]{:S(2)}) copy-start(bf16[2,640,256]{2,1,0:T(8,128)(2,1)} %param.15) | copy-start | bytes 1966084
  0.0 0.7 %copy-start.3 = (s32[40]{0:T(128)S(1)}, s32[40]{0:T(128)}, u32[]{:S(2)}) copy-start(s32[40]{0:T(128)} %param.13) | copy-start | bytes 484
  6.8 0.6 %copy-start.2 = (s32[4,1,40]{2,1,0:T(1,128)}, s32[4,1,40]{2,1,0:T(1,128)S(1)}, u32[]{:S(2)}) copy-start(s32[4,1,40]{2,1,0:T(1,128)S(1)} %shard_map.82.lens) | copy-start | bytes 1924
  20.7 0.9 %copy-start.1 = (bf16[32,4,1024]{2,1,0:T(4,128)(2,1)S(1)}, bf16[32,4,1024]{2,1,0:T(4,128)(2,1)}, u32[]{:S(2)}) copy-start(bf16[32,4,1024]{2,1,0:T(4,128)(2,1)} %shard_map.83.x) | copy-start | bytes 786436
  35.6 0.7 %copy-start.4 = (s32[128]{0:T(128)S(1)}, s32[128]{0:T(128)}, u32[]{:S(2)}) copy-start(s32[128]{0:T(128)} %param.14) | copy-start | bytes 1540

commit v5 on v3

--- a/solution.py
+++ b/solution.py
@@ -218,6 +218,58 @@
                 out[chunk * owners:(chunk + 1) * owners, :, b * LANES:(b + 1) * LANES] = (
                     turned.reshape(owners, slots, LANES)
                 )
+
+
+def legendre(rows, waves_total, orders, got, table, out, first_kept, second_kept):
+    levels = lax.axis_size("lev")
+    bands = lax.axis_size("wide")
+    slots = got.shape[1]
+    device = lax.axis_index("wide") * levels + lax.axis_index("lev")
+    half = bands // 2
+    tall = levels * slots
+
+    def band_fields(w):
+        parts = [got[w * levels + l].astype(jnp.float32) for l in range(levels)]
+        under = jnp.zeros((slots, 2 * rows), jnp.float32)
+        energy = []
+        for l in reversed(range(levels)):
+            energy.append(parts[l][:, :2 * rows] + under)
+            under = under + parts[l][:, 2 * rows:4 * rows]
+        energy = jnp.concatenate(energy[::-1], axis=0)
+        flux = jnp.concatenate([p[:, 4 * rows:6 * rows] for p in parts], axis=0)
+        both = jnp.concatenate([energy, flux], axis=0)
+        return jnp.concatenate([both[:, :rows], both[:, rows:]], axis=0)
+
+    lefts = []
+    for w in range(half):
+        north = band_fields(w)
+        south = band_fields(bands - 1 - w)
+        lefts.append(jnp.concatenate([north + south, north - south], axis=0).astype(jnp.bfloat16))
+    deep = 4 * tall
+    for q in range(slots // 2):
+        first = orders[device * slots + 2 * q]
+        split = waves_total - first
+        for chunk in range(table.shape[2] // LANES):
+            cols = slice(chunk * LANES, (chunk + 1) * LANES)
+            total = jnp.zeros((2 * deep, LANES), jnp.float32)
+            for w in range(half):
+                total = total + jnp.dot(
+                    lefts[w],
+                    table[q, w * rows:(w + 1) * rows, cols],
+                    preferred_element_type=jnp.float32,
+                )
+            even = total[:deep]
+            odd = total[deep:]
+            column = lax.broadcasted_iota(jnp.int32, (deep, LANES), 1) + chunk * LANES
+            shifted = column + split
+            first_kept[...] = jnp.where((column & 1) == 0, even, odd)
+            second_kept[...] = jnp.where((shifted & 1) == 0, even, odd)
+            one = first_kept[pl.ds(2 * q, 4 * levels, stride=slots), :]
+            two = second_kept[pl.ds(2 * q + 1, 4 * levels, stride=slots), :]
+            column = lax.broadcasted_iota(jnp.int32, one.shape, 1) + chunk * LANES
+            result = jnp.where(column < split, one, two)
+            result = jnp.where(column <= waves_total, result, 0.0)
+            out[q, :, cols] = result.astype(out.dtype)
 
 
 def local(u, v, temp, oro, depths, lens, orders, table):
@@ -269,31 +321,19 @@
         oro,
     )
     got = exchange(coefs, ("wide", "lev"), devices, 0)
-    got = got[:, :, :6 * rows].astype(jnp.float32)
-    got = got.reshape(wide_count, lev_count, slots, 3, 2, rows)
-    under = got[:, :, :, 1]
-    below = jnp.cumsum(under[:, ::-1], axis=1)[:, ::-1] - under
-    fields = jnp.stack([got[:, :, :, 0] + below, got[:, :, :, 2]], axis=3)
-    half = wide_count // 2
-    upper = fields[:half]
-    lower = fields[half:][::-1]
-    both = jnp.stack([upper + lower, upper - lower], axis=0).astype(jnp.bfloat16)
-    both = both.transpose(3, 0, 5, 2, 4, 1, 6)
     pairs = slots // 2
     width = table.shape[2]
-    both = both.reshape(pairs, -1, half * rows)
-    product = jnp.einsum("pkj,pjc->pkc", both, table, preferred_element_type=jnp.float32)
-    product = product.reshape(pairs, 4, 2, lev_count, 2, width)
-    mine = lax.dynamic_slice_in_dim(orders, (wide * lev_count + lev) * slots, slots)
-    first = mine.reshape(pairs, 2)[:, :1]
-    column = jnp.arange(width, dtype=jnp.int32)[None]
-    split = waves_total - first
-    chosen = jnp.where(column < split, column % 2, 2 + (column - split) % 2)
-    chosen = jnp.where(column <= waves_total, chosen, 4)[:, None, None, None, :]
-    result = jnp.zeros_like(product[:, 0])
-    for k in range(4):
-        result = jnp.where(chosen == k, product[:, k], result)
-    return result.astype(jnp.bfloat16)
+    vmem = pl.BlockSpec(memory_space=pltpu.VMEM)
+    kept = pltpu.VMEM((4 * lev_count * slots, LANES), jnp.float32)
+    result = pl.pallas_call(
+        functools.partial(legendre, rows, waves_total),
+        out_shape=jax.ShapeDtypeStruct((pairs, 4 * lev_count, width), jnp.bfloat16),
+        in_specs=[smem, vmem, vmem],
+        out_specs=vmem,
+        scratch_shapes=[kept, kept],
+        compiler_params=pltpu.CompilerParams(vmem_limit_bytes=40 * 2**20),
+    )(orders, got, table)
+    return result.reshape(pairs, 2, 2, lev_count, width).transpose(0, 1, 3, 2, 4)
 
 
 def solution(mesh):

time: 37.4 us -> 34.4 us (0.920)
  other arithmetic: 2.15 us -> 0 us
  local copies, waits for them, and re-layouts: 4.59 us -> 2.82 us
  Pallas kernels: 30.1 us -> 31.3 us
    pallas_call x0 -> x1, Pallas kernels: none -> 1.16 us  [local(): pl.pallas_call(functools.partial(legendre, rows, waves_total), out_shape=...]
    another operation x5 -> x0, other arithmetic: 0.81 us -> none  [the longest x2 0.4 us: local(): jnp.stack([upper + lower, upper - lower], axis=0).astype(jnp.bfloat16)]
    unnamed x10, local copies, waits for them, and re-layouts: 2.9 us -> 2.18 us
    convert_element_type x1 -> x0, other arithmetic: 0.65 us -> none  [local(): return result.astype(jnp.bfloat16)]
    reshape x4 -> x2, local copies, waits for them, and re-layouts: 1.13 us -> 0.64 us  [local(): result.reshape(pairs, 2, 2, lev_count, width).transpose(0, 1, 3, 2, 4)]
    transpose x1 -> x0, other arithmetic: 0.42 us -> none  [local(): both = both.transpose(3, 0, 5, 2, 4, 1, 6)]
where the time goes in v5:
time: 34.4 us; the launch traced here: 34.2 us
  Pallas kernels  31.3 us (91%)
  local copies, waits for them, and re-layouts  2.82 us (8%)
    pallas_call x2, Pallas kernels, exchange(): pl.pallas_call(functools.partial(swap, axes), out_shape=jax.ShapeDtypeStr...  16.9 us
    pallas_call x1, Pallas kernels, local(): pl.pallas_call(functools.partial(transform, high, high_pad), grid=(steps,...  13.3 us
    unnamed x10, local copies, waits for them, and re-layouts  2.18 us
    pallas_call x1, Pallas kernels, local(): pl.pallas_call(functools.partial(legendre, rows, waves_total), out_shape=...  1.16 us

profile of v5, /device:TPU:0, one launch (start us, length us, event | category | flops | bytes accessed | tf_op | source)
XLA Modules:
  0.0 34.2 jit_solution(7024500206524729693)
XLA Ops:
  0.0 0.0 copy-start.4
  0.0 0.7 %copy-done.4 = s32[40]{0:T(128)S(1)} copy-done((s32[40]{0:T(128)S(1)}, s32[40]{0:T(128)}, u32[]{:S(2)}) %copy-start.4) | copy-done | bytes 184
  0.7 6.0 %shard_map.82.lens = s32[4,1,40]{2,1,0:T(1,128)S(1)} custom-call(s32[1,1,40]{2,1,0:T(1,128)S(1)} %bitcast.6), custom_call_target="tpu_custom_call" | custom-call | tf_op jit(solution)/shard_map/pallas_call | solution.py:89
  6.7 0.0 copy-start.2
  6.7 0.6 %copy-done.2 = s32[4,1,40]{2,1,0:T(1,128)} copy-done((s32[4,1,40]{2,1,0:T(1,128)}, s32[4,1,40]{2,1,0:T(1,128)S(1)}, u32[]{:S(2)}) %copy-start.2) | copy-done | bytes 664
  7.3 0.0 copy-start.1
  7.3 13.3 %shard_map.83.x = bf16[32,4,1024]{2,1,0:T(4,128)(2,1)} custom-call(s32[4,1,40]{2,1,0:T(1,128)} %copy-done.2, f32[4]{0:T(128)} %depths.1, s32[1,128]{1,0:T(1,128)} %bitcast.5, bf16[1,160,2688]{2,1,0:T(8,128)(2,1)} %u.1, bf16[1,160,2688]{2,1,0:T(8,128)(2,1)} %v.1, bf16[1,160,2688]{2,1,0:T(8,128)(2,1)} %temp.1, bf16[160,2688]{1,0:T(8,128)(2,1)} %oro.1), custom_call_target="tpu_custom_call" | custom-call | tf_op jit(solution)/shard_map/pallas_call | solution.py:294
  20.6 0.0 copy-start
  20.6 0.9 %copy-done = bf16[32,4,1024]{2,1,0:T(4,128)(2,1)S(1)} copy-done((bf16[32,4,1024]{2,1,0:T(4,128)(2,1)S(1)}, bf16[32,4,1024]{2,1,0:T(4,128)(2,1)}, u32[]{:S(2)}) %copy-start) | copy-done | bytes 262168
  21.5 0.0 copy-start.3
  21.5 10.8 %shard_map.84.got = bf16[32,4,1024]{2,1,0:T(4,128)(2,1)S(1)} custom-call(bf16[32,4,1024]{2,1,0:T(4,128)(2,1)S(1)} %copy-done), custom_call_target="tpu_custom_call" | custom-call | tf_op jit(solution)/shard_map/pallas_call | solution.py:89
  32.3 0.0 copy-done.1
  32.4 0.0 copy-done.3
  32.4 1.2 %shard_map.85 = bf16[2,16,256]{2,1,0:T(8,128)(2,1)S(1)} custom-call(s32[128]{0:T(128)S(1)} %copy-done.3, bf16[32,4,1024]{2,1,0:T(4,128)(2,1)S(1)} %shard_map.84.got, bf16[2,640,256]{2,1,0:T(8,128)(2,1)S(1)} %copy-done.1), custom_call_target="tpu_custom_call" | custom-call | tf_op jit(solution)/shard_map/pallas_call | solution.py:328
  33.5 0.6 %copy.11 = bf16[2,2,2,4,256]{4,2,3,1,0:T(2,128)(2,1)} copy(bf16[2,2,2,4,256]{4,3,2,1,0:T(4,128)(2,1)S(1)} %reshape.7) | data formatting | bytes 32768 | tf_op jit(solution)/shard_map/reshape | solution.py:336
  (1 shorter events, 0.0 us)
Async XLA Ops:
  0.0 0.7 %copy-start.4 = (s32[40]{0:T(128)S(1)}, s32[40]{0:T(128)}, u32[]{:S(2)}) copy-start(s32[40]{0:T(128)} %param.13) | copy-start | bytes 484
  6.7 0.6 %copy-start.2 = (s32[4,1,40]{2,1,0:T(1,128)}, s32[4,1,40]{2,1,0:T(1,128)S(1)}, u32[]{:S(2)}) copy-start(s32[4,1,40]{2,1,0:T(1,128)S(1)} %shard_map.82.lens) | copy-start | bytes 1924
  7.3 25.1 %copy-start.1 = (bf16[2,640,256]{2,1,0:T(8,128)(2,1)S(1)}, bf16[2,640,256]{2,1,0:T(8,128)(2,1)}, u32[]{:S(2)}) copy-start(bf16[2,640,256]{2,1,0:T(8,128)(2,1)} %table.1) | copy-start | bytes 1966084
  20.6 0.9 %copy-start = (bf16[32,4,1024]{2,1,0:T(4,128)(2,1)S(1)}, bf16[32,4,1024]{2,1,0:T(4,128)(2,1)}, u32[]{:S(2)}) copy-start(bf16[32,4,1024]{2,1,0:T(4,128)(2,1)} %shard_map.83.x) | copy-start | bytes 786436
  21.5 10.8 %copy-start.3 = (s32[128]{0:T(128)S(1)}, s32[128]{0:T(128)}, u32[]{:S(2)}) copy-start(s32[128]{0:T(128)} %orders.1) | copy-start | bytes 1540

commit v6 on v5

--- a/solution.py
+++ b/solution.py
@@ -69,17 +69,19 @@
             device_id_type=MESH,
         )
 
-    def begin(turn, carry):
-        copy(turn).start()
+    def begin(step, carry):
+        copy(1 + lax.rem(step + count // 2 - 1, count - 1)).start()
         return carry
 
     def finish(turn, carry):
         copy(turn).wait()
         return carry
 
-    lax.fori_loop(1, count, begin, 0)
-    landed[me] = x[0 if shared else me]
+    lax.fori_loop(0, count - 1, begin, 0)
+    own = pltpu.make_async_copy(x.at[0 if shared else me], landed.at[me], send_sem.at[0])
+    own.start()
     lax.fori_loop(1, count, finish, 0)
+    own.wait()
     out[...] = landed[...]
 
 
@@ -89,7 +91,7 @@
     return pl.pallas_call(
         functools.partial(swap, axes),
         out_shape=jax.ShapeDtypeStruct(shape, x.dtype),
-        in_specs=[vmem],
+        in_specs=[pl.BlockSpec(memory_space=pl.ANY)],
         out_specs=vmem,
         scratch_shapes=[
             pltpu.VMEM(shape, x.dtype),
@@ -97,7 +99,7 @@
             pltpu.SemaphoreType.DMA((count,)),
         ],
         compiler_params=pltpu.CompilerParams(
-            collective_id=number, has_side_effects=True, vmem_limit_bytes=24 * 2**20
+            collective_id=number, has_side_effects=True, vmem_limit_bytes=60 * 2**20
         ),
     )(x)
 
@@ -331,7 +333,7 @@
         in_specs=[smem, vmem, vmem],
         out_specs=vmem,
         scratch_shapes=[kept, kept],
-        compiler_params=pltpu.CompilerParams(vmem_limit_bytes=40 * 2**20),
+        compiler_params=pltpu.CompilerParams(vmem_limit_bytes=60 * 2**20),
     )(orders, got, table)
     return result.reshape(pairs, 2, 2, lev_count, width).transpose(0, 1, 3, 2, 4)
 

time: 34.4 us -> 38.4 us (1.12)
  Pallas kernels: 31.3 us -> 36.8 us
  local copies, waits for them, and re-layouts: 2.82 us -> 1.35 us
    pallas_call x2, Pallas kernels: 16.9 us -> 21.2 us  [exchange(): pl.pallas_call(functools.partial(swap, axes), out_shape=jax.ShapeDtypeStr...]
    unnamed x10 -> x0, local copies, waits for them, and re-layouts: 2.18 us -> none
    pallas_call x1, Pallas kernels: 1.16 us -> 2.42 us  [local(): pl.pallas_call(functools.partial(legendre, rows, waves_total), out_shape=...]
    reshape x2, local copies, waits for them, and re-layouts: 0.64 us -> 1.35 us  [local(): result.reshape(pairs, 2, 2, lev_count, width).transpose(0, 1, 3, 2, 4)]
where the time goes in v6:
time: 38.4 us; the launch traced here: 38.2 us
  Pallas kernels  36.8 us (96%)
  local copies, waits for them, and re-layouts  1.35 us (4%)
    pallas_call x2, Pallas kernels, exchange(): pl.pallas_call(functools.partial(swap, axes), out_shape=jax.ShapeDtypeStr...  21.2 us
    pallas_call x1, Pallas kernels, local(): pl.pallas_call(functools.partial(transform, high, high_pad), grid=(steps,...  13.2 us
    pallas_call x1, Pallas kernels, local(): pl.pallas_call(functools.partial(legendre, rows, waves_total), out_shape=...  2.42 us
    reshape x2, local copies, waits for them, and re-layouts, local(): result.reshape(pairs, 2, 2, lev_count, width).transpose(0, 1, 3, 2, 4)  1.35 us

profile of v6, /device:TPU:0, one launch (start us, length us, event | category | flops | bytes accessed | tf_op | source)
XLA Modules:
  0.0 38.2 jit_solution(1577855019089031385)
XLA Ops:
  0.0 6.8 %shard_map.82.lens = s32[4,1,40]{2,1,0:T(1,128)} custom-call(s32[1,1,40]{2,1,0:T(1,128)} %bitcast.6), custom_call_target="tpu_custom_call" | custom-call | tf_op jit(solution)/shard_map/pallas_call | solution.py:91
  6.8 13.2 %shard_map.83.x = bf16[32,4,1024]{2,1,0:T(4,128)(2,1)} custom-call(s32[4,1,40]{2,1,0:T(1,128)} %shard_map.82.lens, f32[4]{0:T(128)} %depths.1, s32[1,128]{1,0:T(1,128)} %bitcast.5, bf16[1,160,2688]{2,1,0:T(8,128)(2,1)} %u.1, bf16[1,160,2688]{2,1,0:T(8,128)(2,1)} %v.1, bf16[1,160,2688]{2,1,0:T(8,128)(2,1)} %temp.1, bf16[160,2688]{1,0:T(8,128)(2,1)} %oro.1), custom_call_target="tpu_custom_call" | custom-call | tf_op jit(solution)/shard_map/pallas_call | solution.py:296
  20.0 14.4 %shard_map.84.got = bf16[32,4,1024]{2,1,0:T(4,128)(2,1)} custom-call(bf16[32,4,1024]{2,1,0:T(4,128)(2,1)} %shard_map.83.x), custom_call_target="tpu_custom_call" | custom-call | tf_op jit(solution)/shard_map/pallas_call | solution.py:91
  34.4 2.4 %shard_map.85 = bf16[2,16,256]{2,1,0:T(8,128)(2,1)} custom-call(s32[128]{0:T(128)} %orders.1, bf16[32,4,1024]{2,1,0:T(4,128)(2,1)} %shard_map.84.got, bf16[2,640,256]{2,1,0:T(8,128)(2,1)} %table.1), custom_call_target="tpu_custom_call" | custom-call | tf_op jit(solution)/shard_map/pallas_call | solution.py:330
  36.8 0.7 %reshape.7 = bf16[2,2,2,4,256]{4,3,2,1,0:T(4,128)(2,1)S(1)} reshape(bf16[2,16,256]{2,1,0:T(8,128)(2,1)} %shard_map.85) | data formatting | bytes 32768 | tf_op jit(solution)/shard_map/reshape | solution.py:338
  37.6 0.6 %copy.11 = bf16[2,2,2,4,256]{4,2,3,1,0:T(2,128)(2,1)} copy(bf16[2,2,2,4,256]{4,3,2,1,0:T(4,128)(2,1)S(1)} %reshape.7) | data formatting | bytes 32768 | tf_op jit(solution)/shard_map/reshape | solution.py:338

commit v7 on v5

--- a/solution.py
+++ b/solution.py
@@ -69,15 +69,15 @@
             device_id_type=MESH,
         )
 
-    def begin(turn, carry):
-        copy(turn).start()
+    def begin(step, carry):
+        copy(1 + lax.rem(step + count // 2 - 1, count - 1)).start()
         return carry
 
     def finish(turn, carry):
         copy(turn).wait()
         return carry
 
-    lax.fori_loop(1, count, begin, 0)
+    lax.fori_loop(0, count - 1, begin, 0)
     landed[me] = x[0 if shared else me]
     lax.fori_loop(1, count, finish, 0)
     out[...] = landed[...]

time: 34.4 us -> 36.9 us (1.073)
  Pallas kernels: 31.3 us -> 33.8 us
    pallas_call x2, Pallas kernels: 16.9 us -> 19.4 us  [exchange(): pl.pallas_call(functools.partial(swap, axes), out_shape=jax.ShapeDtypeStr...]
where the time goes in v7:
time: 36.9 us; the launch traced here: 36.7 us
  Pallas kernels  33.8 us (92%)
  local copies, waits for them, and re-layouts  2.82 us (8%)
    pallas_call x2, Pallas kernels, exchange(): pl.pallas_call(functools.partial(swap, axes), out_shape=jax.ShapeDtypeStr...  19.4 us
    pallas_call x1, Pallas kernels, local(): pl.pallas_call(functools.partial(transform, high, high_pad), grid=(steps,...  13.3 us
    unnamed x10, local copies, waits for them, and re-layouts  2.18 us
    pallas_call x1, Pallas kernels, local(): pl.pallas_call(functools.partial(legendre, rows, waves_total), out_shape=...  1.16 us

profile of v7, /device:TPU:0, one launch (start us, length us, event | category | flops | bytes accessed | tf_op | source)
XLA Modules:
  0.0 36.7 jit_solution(17394649408714796801)
XLA Ops:
  0.0 0.0 copy-start.4
  0.0 0.7 %copy-done.4 = s32[40]{0:T(128)S(1)} copy-done((s32[40]{0:T(128)S(1)}, s32[40]{0:T(128)}, u32[]{:S(2)}) %copy-start.4) | copy-done | bytes 184
  0.7 6.0 %shard_map.82.lens = s32[4,1,40]{2,1,0:T(1,128)S(1)} custom-call(s32[1,1,40]{2,1,0:T(1,128)S(1)} %bitcast.6), custom_call_target="tpu_custom_call" | custom-call | tf_op jit(solution)/shard_map/pallas_call | solution.py:89
  6.7 0.0 copy-start.2
  6.7 0.6 %copy-done.2 = s32[4,1,40]{2,1,0:T(1,128)} copy-done((s32[4,1,40]{2,1,0:T(1,128)}, s32[4,1,40]{2,1,0:T(1,128)S(1)}, u32[]{:S(2)}) %copy-start.2) | copy-done | bytes 664
  7.3 0.0 copy-start.1
  7.3 13.3 %shard_map.83.x = bf16[32,4,1024]{2,1,0:T(4,128)(2,1)} custom-call(s32[4,1,40]{2,1,0:T(1,128)} %copy-done.2, f32[4]{0:T(128)} %depths.1, s32[1,128]{1,0:T(1,128)} %bitcast.5, bf16[1,160,2688]{2,1,0:T(8,128)(2,1)} %u.1, bf16[1,160,2688]{2,1,0:T(8,128)(2,1)} %v.1, bf16[1,160,2688]{2,1,0:T(8,128)(2,1)} %temp.1, bf16[160,2688]{1,0:T(8,128)(2,1)} %oro.1), custom_call_target="tpu_custom_call" | custom-call | tf_op jit(solution)/shard_map/pallas_call | solution.py:294
  20.6 0.0 copy-start
  20.6 0.9 %copy-done = bf16[32,4,1024]{2,1,0:T(4,128)(2,1)S(1)} copy-done((bf16[32,4,1024]{2,1,0:T(4,128)(2,1)S(1)}, bf16[32,4,1024]{2,1,0:T(4,128)(2,1)}, u32[]{:S(2)}) %copy-start) | copy-done | bytes 262168
  21.5 0.0 copy-start.3
  21.5 13.3 %shard_map.84.got = bf16[32,4,1024]{2,1,0:T(4,128)(2,1)S(1)} custom-call(bf16[32,4,1024]{2,1,0:T(4,128)(2,1)S(1)} %copy-done), custom_call_target="tpu_custom_call" | custom-call | tf_op jit(solution)/shard_map/pallas_call | solution.py:89
  34.9 0.0 copy-done.1
  34.9 0.0 copy-done.3
  34.9 1.2 %shard_map.85 = bf16[2,16,256]{2,1,0:T(8,128)(2,1)S(1)} custom-call(s32[128]{0:T(128)S(1)} %copy-done.3, bf16[32,4,1024]{2,1,0:T(4,128)(2,1)S(1)} %shard_map.84.got, bf16[2,640,256]{2,1,0:T(8,128)(2,1)S(1)} %copy-done.1), custom_call_target="tpu_custom_call" | custom-call | tf_op jit(solution)/shard_map/pallas_call | solution.py:328
  36.1 0.6 %copy.11 = bf16[2,2,2,4,256]{4,2,3,1,0:T(2,128)(2,1)} copy(bf16[2,2,2,4,256]{4,3,2,1,0:T(4,128)(2,1)S(1)} %reshape.7) | data formatting | bytes 32768 | tf_op jit(solution)/shard_map/reshape | solution.py:336
  (1 shorter events, 0.0 us)
Async XLA Ops:
  0.0 0.7 %copy-start.4 = (s32[40]{0:T(128)S(1)}, s32[40]{0:T(128)}, u32[]{:S(2)}) copy-start(s32[40]{0:T(128)} %param.13) | copy-start | bytes 484
  6.7 0.6 %copy-start.2 = (s32[4,1,40]{2,1,0:T(1,128)}, s32[4,1,40]{2,1,0:T(1,128)S(1)}, u32[]{:S(2)}) copy-start(s32[4,1,40]{2,1,0:T(1,128)S(1)} %shard_map.82.lens) | copy-start | bytes 1924
  7.3 27.6 %copy-start.1 = (bf16[2,640,256]{2,1,0:T(8,128)(2,1)S(1)}, bf16[2,640,256]{2,1,0:T(8,128)(2,1)}, u32[]{:S(2)}) copy-start(bf16[2,640,256]{2,1,0:T(8,128)(2,1)} %table.1) | copy-start | bytes 1966084
  20.6 0.9 %copy-start = (bf16[32,4,1024]{2,1,0:T(4,128)(2,1)S(1)}, bf16[32,4,1024]{2,1,0:T(4,128)(2,1)}, u32[]{:S(2)}) copy-start(bf16[32,4,1024]{2,1,0:T(4,128)(2,1)} %shard_map.83.x) | copy-start | bytes 786436
  21.5 13.4 %copy-start.3 = (s32[128]{0:T(128)S(1)}, s32[128]{0:T(128)}, u32[]{:S(2)}) copy-start(s32[128]{0:T(128)} %orders.1) | copy-start | bytes 1540
